TPU v7x, 32 devices: a whole 2x2x4 slice. The times are simulated.
32 devices in a mesh: ka: 4 (over y, x), pw: 8 (over z, core).
Axes of the slice: x: 2, y: 2, z: 4, core: 2. Of those that a mesh axis runs over, the one named last changes fastest.
Arguments:
- states_re: bfloat16 [8, 512, 32768], P('ka', None, 'pw'), may hold values from -0.016572815 to 0.016572815
- states_im: bfloat16 [8, 512, 32768], P('ka', None, 'pw'), may hold values from -0.016572815 to 0.016572815
Outputs:
- wilson_lines: float32 [8, 512, 2, 512], P('ka', 'pw')
All inputs are finite; a program needn't handle non-finite values.
Results may differ from a plain program's by a relative error of at most 0.0003.
Values may be sent and summed in bfloat16 or wider, within the bound.
No kernel may reach another device: no remote copies, remote signals or barrier semaphores. Data moves between devices by JAX's collectives and lax.ppermute only.
A program may use at most 128 MiB of HBM per device.

v0:
```python
import functools

import jax
import jax.numpy as jnp
from jax import lax
from jax.experimental import pallas as pl
from jax.experimental.pallas import tpu as pltpu
from jax.sharding import PartitionSpec as P

VMEM_LIMIT = 40 * 1024 * 1024


def halves_of(value):
    high = value.astype(jnp.bfloat16)
    return high, (value - high.astype(jnp.float32)).astype(jnp.bfloat16)


def dot(left, right, across=0):
    return lax.dot_general(left, right, (((1,), (across,)), ((), ())), preferred_element_type=jnp.float32)


def turned(value):
    width = value.shape[1] // 2
    return jnp.concatenate([-value[:, width:], value[:, :width]], 1)


def margin_kernel(steps, pieces, with_left, by_core, *refs):
    refs = list(refs)
    core = refs.pop(0) if by_core else None
    own_re, own_im = refs[:2]
    real_part = jnp.concatenate([ref[...] for ref in refs[2 : 2 + pieces]], 0)
    imag_part = jnp.concatenate([ref[...] for ref in refs[2 + pieces : 2 + 2 * pieces]], 0)
    refs = refs[2 + 2 * pieces :]
    left_high, left_low = refs[:2] if with_left else (None, None)
    outs, total = refs[2 if with_left else 0 : -1], refs[-1]
    step = pl.program_id(0)
    other = jnp.concatenate([jnp.concatenate([real_part, imag_part], 1), jnp.concatenate([imag_part, -real_part], 1)], 0)
    term = dot(jnp.concatenate([own_re[...], own_im[...]], 1), other, 1)

    @pl.when(step == 0)
    def _():
        total[...] = term

    @pl.when(step > 0)
    def _():
        total[...] += term

    @pl.when(step == steps - 1)
    def _():
        if with_left:
            bands = left_high.shape[0]
            value = total[...]
            product = jnp.zeros_like(value)
            for first, factor in ((0, value), (bands, turned(value))):
                high, low = halves_of(factor)
                columns = slice(first, first + bands)
                product += dot(left_high[:, columns], high)
                product += dot(left_high[:, columns], low)
                product += dot(left_low[:, columns], high)
            total[...] = product
        if by_core:
            mine, theirs = outs
            rows = mine.shape[1]
            for chip in range(mine.shape[0]):
                for out, which in ((mine, core[0]), (theirs, 1 - core[0])):
                    first = pl.multiple_of((2 * chip + which) * rows, rows)
                    out[chip] = total[pl.ds(first, rows), :]
        else:
            outs[0][...] = total[...]


def margin_section(states, kpoint, others=None, left=None, core=None):
    _, bands, waves = states[0].shape
    depth = min(1024, waves)
    steps = waves // depth
    own = pl.BlockSpec((None, bands, depth), lambda step: (kpoint, 0, step))
    if others is None:
        width = bands
        other_specs = [pl.BlockSpec((None, bands, depth), lambda step: (kpoint + 1, 0, step))] * 2
        others = states
    else:
        widths = [other.shape[0] // 2 for other in others]
        width = sum(widths)
        other_specs = [pl.BlockSpec((one, depth), lambda step: (0, step)) for one in widths]
        other_specs += [pl.BlockSpec((one, depth), lambda step: (1, step)) for one in widths]
        others = [*others, *others]
    operands, specs = [*states, *others], [own, own, *other_specs]
    if left is not None:
        operands += left
        specs += [pl.BlockSpec((bands, 2 * bands), lambda step: (0, 0))] * 2
    if core is not None:
        operands = [core, *operands]
        specs = [pl.BlockSpec(memory_space=pltpu.SMEM), *specs]
        chips = lax.axis_size("pw") // 2
        shape = (chips, bands // (2 * chips), 2 * width)
        out_shape = [jax.ShapeDtypeStruct(shape, jnp.float32)] * 2
        out_specs = [pl.BlockSpec(shape, lambda step: (0, 0, 0))] * 2
    else:
        out_shape = jax.ShapeDtypeStruct((bands, 2 * width), jnp.float32)
        out_specs = pl.BlockSpec((bands, 2 * width), lambda step: (0, 0))
    return pl.pallas_call(
        functools.partial(margin_kernel, steps, len(other_specs) // 2, left is not None, core is not None),
        grid=(steps,),
        in_specs=specs,
        out_specs=out_specs,
        out_shape=out_shape,
        scratch_shapes=[pltpu.VMEM((bands, 2 * width), jnp.float32)],
        compiler_params=pltpu.CompilerParams(vmem_limit_bytes=VMEM_LIMIT),
        cost_estimate=pl.CostEstimate(flops=0, bytes_accessed=0, transcendentals=0),
    )(*operands)


def split_kernel(value, high, low):
    high[...], low[...] = halves_of(value[...])


def split(value):
    return pl.pallas_call(
        split_kernel,
        out_shape=[jax.ShapeDtypeStruct(value.shape, jnp.bfloat16)] * 2,
        compiler_params=pltpu.CompilerParams(vmem_limit_bytes=VMEM_LIMIT),
    )(value)


def whole_rows(term):
    if len(term) == 1 and len(term[0].shape) == 3:
        rows = term[0][...]
        return jnp.concatenate([rows[0], rows[1]], 0)
    widths = [ref.shape[1] // 2 for ref in term]
    reals = [ref[:, :width] for ref, width in zip(term, widths)]
    imags = [ref[:, width:] for ref, width in zip(term, widths)]
    return jnp.concatenate([jnp.concatenate(reals, 1), jnp.concatenate(imags, 1)], 0)


def whole_piece(refs, place):
    if refs[0].dtype == jnp.bfloat16:
        return refs[0][...], refs[1][...]
    if len(refs) == 1:
        return halves_of(refs[0][...])
    mine, theirs = refs
    chips = mine.shape[0]
    blocks = []
    for chip in range(chips):
        turn = lax.rem(place[0] - chip + chips, chips)
        one, other = mine[turn], theirs[turn]
        blocks += [jnp.where(place[1] == 0, one, other), jnp.where(place[1] == 0, other, one)]
    return halves_of(jnp.concatenate(blocks, 0))


def rows_kernel(tree, place, *refs):
    out = refs[-1]
    terms, matrices = jax.tree.unflatten(tree, refs[:-1])
    flat = whole_rows(terms[0])
    for term in terms[1:]:
        flat = flat + whole_rows(term)
    count = flat.shape[0] // 2
    high, low = halves_of(flat)
    both = jnp.concatenate([high, low], 0)
    for number, matrix in enumerate(matrices):
        first = 0
        for piece in matrix:
            piece_high, piece_low = whole_piece(piece, place)
            product = dot(both, piece_high)
            product = product[: 2 * count] + product[2 * count :] + dot(high, piece_low)
            width = product.shape[1] // 2
            columns = slice(first, first + width)
            out[number, 0, :, columns] = product[:count, :width] - product[count:, width:]
            out[number, 1, :, columns] = product[:count, width:] + product[count:, :width]
            first += width


def rows_times(place, terms, matrices, count, bands):
    flat, tree = jax.tree.flatten((terms, matrices))
    return pl.pallas_call(
        functools.partial(rows_kernel, tree),
        in_specs=[pl.BlockSpec(memory_space=pltpu.SMEM)] + [pl.BlockSpec(memory_space=pltpu.VMEM)] * len(flat),
        out_shape=jax.ShapeDtypeStruct((len(matrices), 2, count, bands), jnp.float32),
        compiler_params=pltpu.CompilerParams(vmem_limit_bytes=24 * 1024 * 1024),
        cost_estimate=pl.CostEstimate(flops=0, bytes_accessed=0, transcendentals=0),
    )(place, *flat)


def pack_kernel(re_ref, im_ref, out):
    out[0] = re_ref[...]
    out[1] = im_ref[...]


def packed_now(states, kpoint, width):
    waves = states[0].shape[2]
    step = min(32, width)
    return pl.pallas_call(
        pack_kernel,
        grid=(width // step,),
        in_specs=[pl.BlockSpec((None, step, waves), lambda i: (kpoint, i, 0))] * 2,
        out_specs=pl.BlockSpec((2, step, waves), lambda i: (0, i, 0)),
        out_shape=jax.ShapeDtypeStruct((2, width, waves), states[0].dtype),
        compiler_params=pltpu.CompilerParams(vmem_limit_bytes=60 * 1024 * 1024),
    )(*states).reshape(2 * width, waves)


def packed(states, kpoint, first, width):
    return jnp.concatenate([s[kpoint, first : first + width] for s in states], 0)


def after(value, earlier):
    return lax.optimization_barrier((value, earlier))[0]


def other_core(block):
    size = lax.axis_size("pw")
    return lax.ppermute(block, "pw", [(i, i ^ 1) for i in range(size)])


def other_chip(block, distance):
    size = lax.axis_size("pw")
    return lax.ppermute(block, "pw", [(i, (i + 2 * distance) % size) for i in range(size)])


def sum_to_rows(mine, theirs):
    chips = mine.shape[0]
    chip = lax.axis_index("pw") // 2
    half = mine + other_core(theirs)

    def block(place):
        return lax.dynamic_index_in_dim(half, place % chips, 0, keepdims=False)

    received = [other_chip(block(chip + d), d) for d in range(1, chips)]
    return sum(received, block(chip))


def rows_to_core(rows):
    chips = lax.axis_size("pw") // 2
    return jnp.stack([rows] + [other_chip(rows, d) for d in range(1, chips)], 0)


def shards(states_re, states_im):
    kcount, bands, _ = states_re.shape
    ka_width = lax.axis_size("ka")
    pw_width = lax.axis_size("pw")
    band_rows = bands // pw_width
    ka_place = lax.axis_index("ka")
    first_band = lax.axis_index("pw") * band_rows
    core = (lax.axis_index("pw") % 2).reshape(1).astype(jnp.int32)
    place = jnp.stack([lax.axis_index("pw") // 2, lax.axis_index("pw") % 2]).astype(jnp.int32)
    quarter = bands // 4
    widths = [2 * quarter, quarter, quarter]
    firsts = [sum(widths[:i]) for i in range(len(widths))]
    to_previous = [(i, (i - 1) % ka_width) for i in range(ka_width)]
    blocks = [packed_now((states_re, states_im), 0, widths[0])]
    blocks += [packed((states_re, states_im), 0, first, width) for first, width in zip(firsts[1:], widths[1:])]

    def send(number, *earlier):
        return lax.ppermute(after(blocks[number], earlier) if earlier else blocks[number], "ka", to_previous)

    arrivals = [send(0)]
    states = after((states_re, states_im), blocks[0])
    last = kcount - 1
    terms = [margin_section(states, k) for k in range(last)]
    arrivals.append(send(1, terms))
    own_margins = [lax.psum(term, "pw") for term in terms]
    before = own_margins[0]
    for k in range(1, last):
        rows = jnp.stack([before[:, :bands], before[:, bands:]], 0)
        before = rows_times(place, [[rows]], [[[own_margins[k]]]], bands, bands)[0]
        before = jnp.concatenate([before[0], before[1]], 1)
        own_margins[k] = before
    left = split(after(before, arrivals[0]))

    rows, span = [], []
    for number in range(len(widths)):
        piece = arrivals[number]
        if number > 0:
            piece = after(piece, half)
        mine, theirs = margin_section(states, last, [piece], left, core)
        if number == 0:
            arrivals.append(send(2, arrivals[0], mine))
        rows.append(sum_to_rows(mine, theirs))
        if number == len(widths) - 1:
            ready = lax.ppermute(after(tuple(rows[:-1]), piece), "ka", [(0, 1)])
            half = rows_to_core(after(rows[-1], ready))
            received = [*ready, lax.ppermute(rows[-1], "ka", [(0, 1)])]
            half_ready = after(half, received[-1])
        else:
            half = half_ready = rows_to_core(rows[-1])
        span.append([half_ready, other_core(half_ready)])

    row_index = lax.broadcasted_iota(jnp.int32, (band_rows, bands), 0) + first_band
    col_index = lax.broadcasted_iota(jnp.int32, (band_rows, bands), 1)
    eye_real = jnp.where((row_index == col_index) & (ka_place == 0), 1.0, 0.0).astype(jnp.float32)
    starts = [[jnp.stack([eye_real, jnp.zeros_like(eye_real)], 0)], received]
    for number in range(1, ka_width - 1):
        line = rows_times(place, starts[-1:], [span], band_rows, bands)[0]
        starts.append([lax.ppermute(line, "ka", [(number, number + 1)])])

    margins = [[[margin]] for margin in own_margins]
    margins[-1] = [left]
    lines = rows_times(place, starts, margins + [span], band_rows, bands)
    return jnp.moveaxis(lines, 1, 2)


def solution(mesh):
    in_specs = (P("ka", None, "pw"), P("ka", None, "pw"))
    out_specs = P("ka", "pw", None, None)
    return jax.shard_map(shards, mesh=mesh, in_specs=in_specs, out_specs=out_specs, check_vma=False)
```

profile of v0, /device:TPU:6, one launch (start us, length us, event | category | flops | bytes accessed | tf_op | source)
XLA Modules:
  0.0 271.7 jit_solution(17864923306611387252)
XLA Ops:
  6.5 6.6 %shard_map.28 = bf16[2,256,4096]{2,1,0:T(8,128)(2,1)} custom-call(bf16[2,512,4096]{2,1,0:T(8,128)(2,1)} %refs_1_.3, bf16[2,512,4096]{2,1,0:T(8,128)(2,1)} %refs_2_.3), custom_call_target="tpu_custom_call" | custom-call | tf_op jit(solution)/shard_map/pallas_call | solution.py:191
  13.7 3.4 %copy-done = bf16[2,512,4096]{2,1,0:T(8,128)(2,1)S(1)} copy-done((bf16[2,512,4096]{2,1,0:T(8,128)(2,1)S(1)}, bf16[2,512,4096]{2,1,0:T(8,128)(2,1)}, u32[]{:S(2)}) %copy-start) | copy-done | bytes 8388632
  17.0 13.6 %shard_map.29 = f32[512,1024]{1,0:T(8,128)} custom-call(bf16[2,512,4096]{2,1,0:T(8,128)(2,1)S(1)} %copy-done, bf16[2,512,4096]{2,1,0:T(8,128)(2,1)} %refs_2_.3, bf16[2,512,4096]{2,1,0:T(8,128)(2,1)S(1)} %copy-done, bf16[2,512,4096]{2,1,0:T(8,128)(2,1)} %refs_2_.3), custom_call_target="tpu_custom_call" | custom-call | tf_op jit(solution)/shard_map/pallas_call | solution.py:101
  30.6 4.0 %slice_bitcast_fusion = (bf16[128,4096]{1,0:T(8,128)(2,1)}, bf16[128,4096]{1,0:T(8,128)(2,1)S(1)}, bf16[128,4096]{1,0:T(8,128)(2,1)S(1)}, bf16[128,4096]{1,0:T(8,128)(2,1)}) fusion(bf16[2,512,4096]{2,1,0:T(8,128)(2,1)} %refs_2_.3, bf16[2,512,4096]{2,1,0:T(8,128)(2,1)} %refs_1_.3), kind=kLoop, calls=%fused_computation.2 | loop fusion | bytes 8388608 | tf_op jit(solution)/shard_map/squeeze | solution.py:202
  34.6 1.5 pad_maximum_fusion
  36.2 1.5 collective-permute-start.5
  37.7 64.8 %all-reduce.3.cloned.1.call-done.value = f32[512,1024]{1,0:T(8,128)} async-done(((f32[512,1024]{1,0:T(8,128)}), f32[512,1024]{1,0:T(8,128)}) %all-reduce.3.cloned.1.call-update) | async-done | bytes 2097168 | tf_op jit(solution)/shard_map/psum | solution.py:260
  102.5 5.3 %collective-permute-done.refs_3_.refs_4_ = bf16[512,4096]{1,0:T(8,128)(2,1)} collective-permute-done((bf16[512,4096]{1,0:T(8,128)(2,1)}, bf16[512,4096]{1,0:T(8,128)(2,1)}, u32[]{:S(2)}, u32[]{:S(2)}) %collective-permute-start) | collective-permute-done | bytes 4194336 | tf_op jit(solution)/shard_map/ppermute | solution.py:253
  107.8 1.6 copy-done.11
  109.7 10.0 %shard_map.31 = (f32[4,64,512]{2,1,0:T(8,128)S(1)}, f32[4,64,512]{2,1,0:T(8,128)S(1)}) custom-call(s32[1]{0:T(128)} %bitcast.1.refs_0_, bf16[2,512,4096]{2,1,0:T(8,128)(2,1)} %refs_1_.3, bf16[2,512,4096]{2,1,0:T(8,128)(2,1)} %refs_2_.3, bf16[512,4096]{1,0:T(8,128)(2,1)} %collective-permute-done.refs_3_.refs_4_, ...), custom_call_target="tpu_custom_call" | custom-call | tf_op jit(solution)/shard_map/pallas_call | solution.py:101
  119.8 1.6 pad_maximum_fusion.1
  121.8 1.1 add.113
  123.0 3.7 %collective-permute-start.4 = (f32[64,512]{1,0:T(8,128)S(1)}, f32[64,512]{1,0:T(8,128)S(1)}, u32[]{:S(2)}, u32[]{:S(2)}) collective-permute-start(f32[64,512]{1,0:T(8,128)S(1)} %get-tuple-element.48), channel_id=1, source_target_pairs={{0,6},{1,7},{2,0},{3,1},{4,2},{5,3},{6,4},{7,5},{8,14},{9,15},{10,... | collective-permute-start | bytes 393224 | tf_op jit(solution)/shard_map/ppermute | solution.py:216
  127.6 2.9 %collective-permute-done.4 = f32[64,512]{1,0:T(8,128)S(1)} collective-permute-done((f32[64,512]{1,0:T(8,128)S(1)}, f32[64,512]{1,0:T(8,128)S(1)}, u32[]{:S(2)}, u32[]{:S(2)}) %collective-permute-start.4) | collective-permute-done | bytes 131104 | tf_op jit(solution)/shard_map/ppermute | solution.py:216
  130.6 7.7 %collective-permute-done.3 = f32[64,512]{1,0:T(8,128)S(1)} collective-permute-done((f32[64,512]{1,0:T(8,128)S(1)}, f32[64,512]{1,0:T(8,128)S(1)}, u32[]{:S(2)}, u32[]{:S(2)}) %collective-permute-start.3) | collective-permute-done | bytes 131104 | tf_op jit(solution)/shard_map/ppermute | solution.py:216
  138.4 1.5 collective-permute-start.8
  139.8 1.1 collective-permute-start.7
  141.0 1.9 collective-permute-start.6
  142.9 1.2 collective-permute-done.8
  144.1 8.3 %collective-permute-done.7 = f32[64,512]{1,0:T(8,128)S(1)} collective-permute-done((f32[64,512]{1,0:T(8,128)S(1)}, f32[64,512]{1,0:T(8,128)S(1)}, u32[]{:S(2)}, u32[]{:S(2)}) %collective-permute-start.7) | collective-permute-done | bytes 131104 | tf_op jit(solution)/shard_map/ppermute | solution.py:216
  152.7 3.4 %copy-done.1 = bf16[2,512,4096]{2,1,0:T(8,128)(2,1)S(1)} copy-done((bf16[2,512,4096]{2,1,0:T(8,128)(2,1)S(1)}, bf16[2,512,4096]{2,1,0:T(8,128)(2,1)}, u32[]{:S(2)}) %copy-start.1) | copy-done | bytes 8388632
  156.1 6.5 %shard_map.32 = (f32[4,64,256]{2,1,0:T(8,128)S(1)}, f32[4,64,256]{2,1,0:T(8,128)S(1)}) custom-call(s32[1]{0:T(128)} %bitcast.1.refs_0_, bf16[2,512,4096]{2,1,0:T(8,128)(2,1)S(1)} %copy-done.1, bf16[2,512,4096]{2,1,0:T(8,128)(2,1)} %refs_2_.3, bf16[256,4096]{1,0:T(8,128)(2,1)} %collective-permute-done.5.refs_3_.refs_4_, ...), custom_call_target="tpu_custom_call" | custom-call | tf_op jit(solution)/shard_map/pallas_call | solution.py:101
  162.7 1.5 collective-permute-done.9
  164.3 3.6 %collective-permute-start.12 = (f32[64,256]{1,0:T(8,128)S(1)}, f32[64,256]{1,0:T(8,128)S(1)}, u32[]{:S(2)}, u32[]{:S(2)}) collective-permute-start(f32[64,256]{1,0:T(8,128)S(1)} %get-tuple-element.54), channel_id=1, source_target_pairs={{0,6},{1,7},{2,0},{3,1},{4,2},{5,3},{6,4},{7,5},{8,14},{9,15},{10,... | collective-permute-start | bytes 196616 | tf_op jit(solution)/shard_map/ppermute | solution.py:216
  167.9 1.0 collective-permute-start.10
  168.9 1.5 collective-permute-done.12
  170.4 4.3 %collective-permute-done.11 = f32[64,256]{1,0:T(8,128)S(1)} collective-permute-done((f32[64,256]{1,0:T(8,128)S(1)}, f32[64,256]{1,0:T(8,128)S(1)}, u32[]{:S(2)}, u32[]{:S(2)}) %collective-permute-start.11) | collective-permute-done | bytes 65568 | tf_op jit(solution)/shard_map/ppermute | solution.py:216
  174.7 1.9 collective-permute-start.16
  176.6 1.9 collective-permute-start.14
  178.6 1.2 collective-permute-done.16
  179.7 3.9 %collective-permute-done.15 = f32[64,256]{1,0:T(8,128)S(1)} collective-permute-done((f32[64,256]{1,0:T(8,128)S(1)}, f32[64,256]{1,0:T(8,128)S(1)}, u32[]{:S(2)}, u32[]{:S(2)}) %collective-permute-start.15) | collective-permute-done | bytes 65568 | tf_op jit(solution)/shard_map/ppermute | solution.py:216
  183.6 12.9 %collective-permute-done.13.refs_3_.refs_4_ = bf16[256,4096]{1,0:T(8,128)(2,1)} collective-permute-done((bf16[256,4096]{1,0:T(8,128)(2,1)}, bf16[256,4096]{1,0:T(8,128)(2,1)}, u32[]{:S(2)}, u32[]{:S(2)}) %collective-permute-start.13) | collective-permute-done | bytes 2097184 | tf_op jit(solution)/shard_map/ppermute | solution.py:253
  196.5 6.5 %shard_map.33 = (f32[4,64,256]{2,1,0:T(8,128)S(1)}, f32[4,64,256]{2,1,0:T(8,128)S(1)}) custom-call(s32[1]{0:T(128)} %bitcast.1.refs_0_, bf16[2,512,4096]{2,1,0:T(8,128)(2,1)S(1)} %copy-done.1, bf16[2,512,4096]{2,1,0:T(8,128)(2,1)} %refs_2_.3, bf16[256,4096]{1,0:T(8,128)(2,1)} %collective-permute-done.13.refs_3_.refs_4_, ...), custom_call_target="tpu_custom_call" | custom-call | tf_op jit(solution)/shard_map/pallas_call | solution.py:101
  203.1 1.5 collective-permute-done.19
  204.7 3.6 %collective-permute-start.22 = (f32[64,256]{1,0:T(8,128)S(1)}, f32[64,256]{1,0:T(8,128)S(1)}, u32[]{:S(2)}, u32[]{:S(2)}) collective-permute-start(f32[64,256]{1,0:T(8,128)S(1)} %get-tuple-element.51), channel_id=1, source_target_pairs={{0,6},{1,7},{2,0},{3,1},{4,2},{5,3},{6,4},{7,5},{8,14},{9,15},{10,... | collective-permute-start | bytes 196616 | tf_op jit(solution)/shard_map/ppermute | solution.py:216
  211.5 3.6 %collective-permute-done.21 = f32[64,256]{1,0:T(8,128)S(1)} collective-permute-done((f32[64,256]{1,0:T(8,128)S(1)}, f32[64,256]{1,0:T(8,128)S(1)}, u32[]{:S(2)}, u32[]{:S(2)}) %collective-permute-start.21) | collective-permute-done | bytes 65568 | tf_op jit(solution)/shard_map/ppermute | solution.py:216
  215.2 2.1 collective-permute-start.28
  217.3 1.9 collective-permute-start.26
  219.2 1.1 collective-permute-done.28
  220.9 3.2 %collective-permute-done.27 = f32[64,256]{1,0:T(8,128)S(1)} collective-permute-done((f32[64,256]{1,0:T(8,128)S(1)}, f32[64,256]{1,0:T(8,128)S(1)}, u32[]{:S(2)}, u32[]{:S(2)}) %collective-permute-start.27) | collective-permute-done | bytes 65568 | tf_op jit(solution)/shard_map/ppermute | solution.py:216
  224.3 1.4 collective-permute-done.29.refs_8_.refs_6_.refs_13_
  225.8 1.9 shard_map.34
  228.4 1.4 collective-permute-start.30
  232.6 2.3 shard_map.35
  234.9 1.3 collective-permute-start.31
  236.3 20.7 %collective-permute-done.31.refs_5_ = f32[2,64,512]{2,1,0:T(8,128)} collective-permute-done((f32[2,64,512]{2,1,0:T(8,128)}, f32[2,64,512]{2,1,0:T(8,128)}, u32[]{:S(2)}, u32[]{:S(2)}) %collective-permute-start.31) | collective-permute-done | bytes 262176 | tf_op jit(solution)/shard_map/ppermute | solution.py:293
  261.6 2.1 shard_map.36
  263.7 1.2 copy.3
  (84 shorter events, 15.3 us)
Async XLA Ops:
  6.5 96.0 %all-reduce.3.cloned.1.call-start = ((), (), s32[]{:S(2)}) async-start(), calls=%async_computation | async-start | bytes 4194304 | tf_op jit(solution)/shard_map/psum | solution.py:260
  13.1 94.7 %collective-permute-start = (bf16[512,4096]{1,0:T(8,128)(2,1)}, bf16[512,4096]{1,0:T(8,128)(2,1)}, u32[]{:S(2)}, u32[]{:S(2)}) collective-permute-start(bf16[512,4096]{1,0:T(8,128)(2,1)} %bitcast.63), channel_id=1, source_target_pairs={{0,24},{8,0},{16,8},{24,16},{1,25},{9,1},{17,9},{25,17},{2,26},{10... | collective-permute-start | bytes 12582920 | tf_op jit(solution)/shard_map/ppermute | solution.py:253
  13.7 3.4 %copy-start = (bf16[2,512,4096]{2,1,0:T(8,128)(2,1)S(1)}, bf16[2,512,4096]{2,1,0:T(8,128)(2,1)}, u32[]{:S(2)}) copy-start(bf16[2,512,4096]{2,1,0:T(8,128)(2,1)} %refs_1_.3) | copy-start | bytes 25165828
  36.2 116.5 %collective-permute-start.5 = (bf16[256,4096]{1,0:T(8,128)(2,1)}, bf16[256,4096]{1,0:T(8,128)(2,1)}, u32[]{:S(2)}, u32[]{:S(2)}) collective-permute-start(bf16[256,4096]{1,0:T(8,128)(2,1)} %pad_maximum_fusion), channel_id=1, source_target_pairs={{0,24},{8,0},{16,8},{24,16},{1,25},{9,1},{17,9},{25,17},{2,26},{10... | collective-permute-start | bytes 6291464 | tf_op jit(solution)/shard_map/ppermute | solution.py:253
  107.8 1.6 copy-start.11
  109.7 10.1 %copy-start.16 = (bf16[128,4096]{1,0:T(8,128)(2,1)S(1)}, bf16[128,4096]{1,0:T(8,128)(2,1)}, u32[]{:S(2)}) copy-start(bf16[128,4096]{1,0:T(8,128)(2,1)} %get-tuple-element.45) | copy-start | bytes 3145732
  109.7 10.1 %copy-start.17 = (bf16[128,4096]{1,0:T(8,128)(2,1)S(1)}, bf16[128,4096]{1,0:T(8,128)(2,1)}, u32[]{:S(2)}) copy-start(bf16[128,4096]{1,0:T(8,128)(2,1)} %get-tuple-element.57) | copy-start | bytes 3145732
  119.7 2.1 collective-permute-start.1
  121.4 75.2 %collective-permute-start.13 = (bf16[256,4096]{1,0:T(8,128)(2,1)}, bf16[256,4096]{1,0:T(8,128)(2,1)}, u32[]{:S(2)}, u32[]{:S(2)}) collective-permute-start(bf16[256,4096]{1,0:T(8,128)(2,1)} %pad_maximum_fusion.1), channel_id=1, source_target_pairs={{0,24},{8,0},{16,8},{24,16},{1,25},{9,1},{17,9},{25,17},{2,26},{10... | collective-permute-start | bytes 6291464 | tf_op jit(solution)/shard_map/ppermute | solution.py:253
  123.0 7.6 %collective-permute-start.4 = (f32[64,512]{1,0:T(8,128)S(1)}, f32[64,512]{1,0:T(8,128)S(1)}, u32[]{:S(2)}, u32[]{:S(2)}) collective-permute-start(f32[64,512]{1,0:T(8,128)S(1)} %get-tuple-element.48), channel_id=1, source_target_pairs={{0,6},{1,7},{2,0},{3,1},{4,2},{5,3},{6,4},{7,5},{8,14},{9,15},{10,... | collective-permute-start | bytes 393224 | tf_op jit(solution)/shard_map/ppermute | solution.py:216
  126.6 11.7 %collective-permute-start.3 = (f32[64,512]{1,0:T(8,128)S(1)}, f32[64,512]{1,0:T(8,128)S(1)}, u32[]{:S(2)}, u32[]{:S(2)}) collective-permute-start(f32[64,512]{1,0:T(8,128)S(1)} %get-tuple-element.49), channel_id=1, source_target_pairs={{0,4},{1,5},{2,6},{3,7},{4,0},{5,1},{6,2},{7,3},{8,12},{9,13},{10,... | collective-permute-start | bytes 393224 | tf_op jit(solution)/shard_map/ppermute | solution.py:216
  126.6 11.7 %collective-permute-start.2 = (f32[64,512]{1,0:T(8,128)S(1)}, f32[64,512]{1,0:T(8,128)S(1)}, u32[]{:S(2)}, u32[]{:S(2)}) collective-permute-start(f32[64,512]{1,0:T(8,128)S(1)} %get-tuple-element.47), channel_id=1, source_target_pairs={{0,2},{1,3},{2,4},{3,5},{4,6},{5,7},{6,0},{7,1},{8,10},{9,11},{10,... | collective-permute-start | bytes 393224 | tf_op jit(solution)/shard_map/ppermute | solution.py:216
  138.4 5.7 %collective-permute-start.8 = (f32[64,512]{1,0:T(8,128)S(1)}, f32[64,512]{1,0:T(8,128)S(1)}, u32[]{:S(2)}, u32[]{:S(2)}) collective-permute-start(f32[64,512]{1,0:T(8,128)S(1)} %fusion.1), channel_id=1, source_target_pairs={{0,6},{1,7},{2,0},{3,1},{4,2},{5,3},{6,4},{7,5},{8,14},{9,15},{10,... | collective-permute-start | bytes 393224 | tf_op jit(solution)/shard_map/ppermute | solution.py:216
  139.8 12.5 %collective-permute-start.7 = (f32[64,512]{1,0:T(8,128)S(1)}, f32[64,512]{1,0:T(8,128)S(1)}, u32[]{:S(2)}, u32[]{:S(2)}) collective-permute-start(f32[64,512]{1,0:T(8,128)S(1)} %fusion.1), channel_id=1, source_target_pairs={{0,4},{1,5},{2,6},{3,7},{4,0},{5,1},{6,2},{7,3},{8,12},{9,13},{10,... | collective-permute-start | bytes 393224 | tf_op jit(solution)/shard_map/ppermute | solution.py:216
  141.0 11.4 %collective-permute-start.6 = (f32[64,512]{1,0:T(8,128)S(1)}, f32[64,512]{1,0:T(8,128)S(1)}, u32[]{:S(2)}, u32[]{:S(2)}) collective-permute-start(f32[64,512]{1,0:T(8,128)S(1)} %fusion.1), channel_id=1, source_target_pairs={{0,2},{1,3},{2,4},{3,5},{4,6},{5,7},{6,0},{7,1},{8,10},{9,11},{10,... | collective-permute-start | bytes 393224 | tf_op jit(solution)/shard_map/ppermute | solution.py:216
  152.7 3.4 %copy-start.1 = (bf16[2,512,4096]{2,1,0:T(8,128)(2,1)S(1)}, bf16[2,512,4096]{2,1,0:T(8,128)(2,1)}, u32[]{:S(2)}) copy-start(bf16[2,512,4096]{2,1,0:T(8,128)(2,1)} %refs_1_.3) | copy-start | bytes 25165828
  162.6 1.6 collective-permute-start.9
  164.3 6.1 %collective-permute-start.12 = (f32[64,256]{1,0:T(8,128)S(1)}, f32[64,256]{1,0:T(8,128)S(1)}, u32[]{:S(2)}, u32[]{:S(2)}) collective-permute-start(f32[64,256]{1,0:T(8,128)S(1)} %get-tuple-element.54), channel_id=1, source_target_pairs={{0,6},{1,7},{2,0},{3,1},{4,2},{5,3},{6,4},{7,5},{8,14},{9,15},{10,... | collective-permute-start | bytes 196616 | tf_op jit(solution)/shard_map/ppermute | solution.py:216
  167.9 6.8 %collective-permute-start.11 = (f32[64,256]{1,0:T(8,128)S(1)}, f32[64,256]{1,0:T(8,128)S(1)}, u32[]{:S(2)}, u32[]{:S(2)}) collective-permute-start(f32[64,256]{1,0:T(8,128)S(1)} %get-tuple-element.55), channel_id=1, source_target_pairs={{0,4},{1,5},{2,6},{3,7},{4,0},{5,1},{6,2},{7,3},{8,12},{9,13},{10,... | collective-permute-start | bytes 196616 | tf_op jit(solution)/shard_map/ppermute | solution.py:216
  167.9 6.8 %collective-permute-start.10 = (f32[64,256]{1,0:T(8,128)S(1)}, f32[64,256]{1,0:T(8,128)S(1)}, u32[]{:S(2)}, u32[]{:S(2)}) collective-permute-start(f32[64,256]{1,0:T(8,128)S(1)} %get-tuple-element.53), channel_id=1, source_target_pairs={{0,2},{1,3},{2,4},{3,5},{4,6},{5,7},{6,0},{7,1},{8,10},{9,11},{10,... | collective-permute-start | bytes 196616 | tf_op jit(solution)/shard_map/ppermute | solution.py:216
  174.7 5.0 %collective-permute-start.16 = (f32[64,256]{1,0:T(8,128)S(1)}, f32[64,256]{1,0:T(8,128)S(1)}, u32[]{:S(2)}, u32[]{:S(2)}) collective-permute-start(f32[64,256]{1,0:T(8,128)S(1)} %fusion.7), channel_id=1, source_target_pairs={{0,6},{1,7},{2,0},{3,1},{4,2},{5,3},{6,4},{7,5},{8,14},{9,15},{10,... | collective-permute-start | bytes 196616 | tf_op jit(solution)/shard_map/ppermute | solution.py:216
  176.6 6.9 %collective-permute-start.15 = (f32[64,256]{1,0:T(8,128)S(1)}, f32[64,256]{1,0:T(8,128)S(1)}, u32[]{:S(2)}, u32[]{:S(2)}) collective-permute-start(f32[64,256]{1,0:T(8,128)S(1)} %fusion.7), channel_id=1, source_target_pairs={{0,4},{1,5},{2,6},{3,7},{4,0},{5,1},{6,2},{7,3},{8,12},{9,13},{10,... | collective-permute-start | bytes 196616 | tf_op jit(solution)/shard_map/ppermute | solution.py:216
  176.6 6.9 %collective-permute-start.14 = (f32[64,256]{1,0:T(8,128)S(1)}, f32[64,256]{1,0:T(8,128)S(1)}, u32[]{:S(2)}, u32[]{:S(2)}) collective-permute-start(f32[64,256]{1,0:T(8,128)S(1)} %fusion.7), channel_id=1, source_target_pairs={{0,2},{1,3},{2,4},{3,5},{4,6},{5,7},{6,0},{7,1},{8,10},{9,11},{10,... | collective-permute-start | bytes 196616 | tf_op jit(solution)/shard_map/ppermute | solution.py:216
  203.0 1.6 collective-permute-start.19
  204.7 6.1 %collective-permute-start.22 = (f32[64,256]{1,0:T(8,128)S(1)}, f32[64,256]{1,0:T(8,128)S(1)}, u32[]{:S(2)}, u32[]{:S(2)}) collective-permute-start(f32[64,256]{1,0:T(8,128)S(1)} %get-tuple-element.51), channel_id=1, source_target_pairs={{0,6},{1,7},{2,0},{3,1},{4,2},{5,3},{6,4},{7,5},{8,14},{9,15},{10,... | collective-permute-start | bytes 196616 | tf_op jit(solution)/shard_map/ppermute | solution.py:216
  208.3 6.8 %collective-permute-start.21 = (f32[64,256]{1,0:T(8,128)S(1)}, f32[64,256]{1,0:T(8,128)S(1)}, u32[]{:S(2)}, u32[]{:S(2)}) collective-permute-start(f32[64,256]{1,0:T(8,128)S(1)} %get-tuple-element.52), channel_id=1, source_target_pairs={{0,4},{1,5},{2,6},{3,7},{4,0},{5,1},{6,2},{7,3},{8,12},{9,13},{10,... | collective-permute-start | bytes 196616 | tf_op jit(solution)/shard_map/ppermute | solution.py:216
  208.3 6.8 %collective-permute-start.20 = (f32[64,256]{1,0:T(8,128)S(1)}, f32[64,256]{1,0:T(8,128)S(1)}, u32[]{:S(2)}, u32[]{:S(2)}) collective-permute-start(f32[64,256]{1,0:T(8,128)S(1)} %get-tuple-element.50), channel_id=1, source_target_pairs={{0,2},{1,3},{2,4},{3,5},{4,6},{5,7},{6,0},{7,1},{8,10},{9,11},{10,... | collective-permute-start | bytes 196616 | tf_op jit(solution)/shard_map/ppermute | solution.py:216
  209.3 15.0 %collective-permute-start.24 = (f32[4,64,512]{2,1,0:T(8,128)S(1)}, f32[4,64,512]{2,1,0:T(8,128)S(1)}, u32[]{:S(2)}, u32[]{:S(2)}) collective-permute-start(f32[4,64,512]{2,1,0:T(8,128)S(1)} %pad_maximum_fusion.2.refs_3_.refs_1_.refs_8_), channel_id=1, source_target_pairs={{0,1},{1,0},{2,3},{3,2},{4,5},{5,4},{6,7},{7,6},{8,9},{9,8},{10,11... | collective-permute-start | bytes 1572872 | tf_op jit(solution)/shard_map/ppermute | solution.py:211
  209.3 5.8 %collective-permute-start.17 = (f32[64,512]{1,0:T(8,128)S(1)}, f32[64,512]{1,0:T(8,128)S(1)}, u32[]{:S(2)}, u32[]{:S(2)}) collective-permute-start(f32[64,512]{1,0:T(8,128)S(1)} %fusion.1), channel_id=1, source_target_pairs={{0,8},{1,9},{2,10},{3,11},{4,12},{5,13},{6,14},{7,15}} | collective-permute-start | bytes 393224 | tf_op jit(solution)/shard_map/ppermute | solution.py:279
  210.8 4.3 %collective-permute-start.18 = (f32[64,256]{1,0:T(8,128)S(1)}, f32[64,256]{1,0:T(8,128)S(1)}, u32[]{:S(2)}, u32[]{:S(2)}) collective-permute-start(f32[64,256]{1,0:T(8,128)S(1)} %fusion.7), channel_id=1, source_target_pairs={{0,8},{1,9},{2,10},{3,11},{4,12},{5,13},{6,14},{7,15}} | collective-permute-start | bytes 196616 | tf_op jit(solution)/shard_map/ppermute | solution.py:279
  215.1 13.2 %copy-start.12 = (f32[64,256]{1,0:T(8,128)}, f32[64,256]{1,0:T(8,128)S(1)}, u32[]{:S(2)}) copy-start(f32[64,256]{1,0:T(8,128)S(1)} %collective-permute-done.18.refs_1_.refs_2_) | copy-start | bytes 196612
  215.2 5.1 %collective-permute-start.28 = (f32[64,256]{1,0:T(8,128)S(1)}, f32[64,256]{1,0:T(8,128)S(1)}, u32[]{:S(2)}, u32[]{:S(2)}) collective-permute-start(f32[64,256]{1,0:T(8,128)S(1)} %fusion.5), channel_id=1, source_target_pairs={{0,6},{1,7},{2,0},{3,1},{4,2},{5,3},{6,4},{7,5},{8,14},{9,15},{10,... | collective-permute-start | bytes 196616 | tf_op jit(solution)/shard_map/ppermute | solution.py:216
  217.3 6.8 %collective-permute-start.27 = (f32[64,256]{1,0:T(8,128)S(1)}, f32[64,256]{1,0:T(8,128)S(1)}, u32[]{:S(2)}, u32[]{:S(2)}) collective-permute-start(f32[64,256]{1,0:T(8,128)S(1)} %fusion.5), channel_id=1, source_target_pairs={{0,4},{1,5},{2,6},{3,7},{4,0},{5,1},{6,2},{7,3},{8,12},{9,13},{10,... | collective-permute-start | bytes 196616 | tf_op jit(solution)/shard_map/ppermute | solution.py:216
  217.3 6.8 %collective-permute-start.26 = (f32[64,256]{1,0:T(8,128)S(1)}, f32[64,256]{1,0:T(8,128)S(1)}, u32[]{:S(2)}, u32[]{:S(2)}) collective-permute-start(f32[64,256]{1,0:T(8,128)S(1)} %fusion.5), channel_id=1, source_target_pairs={{0,2},{1,3},{2,4},{3,5},{4,6},{5,7},{6,0},{7,1},{8,10},{9,11},{10,... | collective-permute-start | bytes 196616 | tf_op jit(solution)/shard_map/ppermute | solution.py:216
  219.2 5.1 %collective-permute-start.25 = (f32[4,64,256]{2,1,0:T(8,128)S(1)}, f32[4,64,256]{2,1,0:T(8,128)S(1)}, u32[]{:S(2)}, u32[]{:S(2)}) collective-permute-start(f32[4,64,256]{2,1,0:T(8,128)S(1)} %pad_maximum_fusion.3.refs_5_.refs_3_.refs_10_), channel_id=1, source_target_pairs={{0,1},{1,0},{2,3},{3,2},{4,5},{5,4},{6,7},{7,6},{8,9},{9,8},{10,11... | collective-permute-start | bytes 786440 | tf_op jit(solution)/shard_map/ppermute | solution.py:211
  220.2 3.9 %collective-permute-start.23 = (f32[64,256]{1,0:T(8,128)S(1)}, f32[64,256]{1,0:T(8,128)S(1)}, u32[]{:S(2)}, u32[]{:S(2)}) collective-permute-start(f32[64,256]{1,0:T(8,128)S(1)} %fusion.5), channel_id=1, source_target_pairs={{0,8},{1,9},{2,10},{3,11},{4,12},{5,13},{6,14},{7,15}} | collective-permute-start | bytes 196616 | tf_op jit(solution)/shard_map/ppermute | solution.py:281
  224.1 4.2 %copy-start.14 = (f32[64,256]{1,0:T(8,128)}, f32[64,256]{1,0:T(8,128)S(1)}, u32[]{:S(2)}) copy-start(f32[64,256]{1,0:T(8,128)S(1)} %collective-permute-done.23.refs_2_.refs_3_) | copy-start | bytes 196612
  224.1 1.6 collective-permute-start.29
  224.3 3.3 %copy-start.5 = (f32[4,64,256]{2,1,0:T(8,128)}, f32[4,64,256]{2,1,0:T(8,128)S(1)}, u32[]{:S(2)}) copy-start(f32[4,64,256]{2,1,0:T(8,128)S(1)} %collective-permute-done.25.refs_6_.refs_4_.refs_11_) | copy-start | bytes 786436
  225.8 2.6 copy-start.8
  228.4 1.4 collective-permute-start.30
  229.7 1.0 copy-start.3
  230.7 0.9 copy-start.6
  231.6 0.9 copy-start.9
  234.9 22.2 %collective-permute-start.31 = (f32[2,64,512]{2,1,0:T(8,128)}, f32[2,64,512]{2,1,0:T(8,128)}, u32[]{:S(2)}, u32[]{:S(2)}) collective-permute-start(f32[2,64,512]{2,1,0:T(8,128)} %bitcast.32), channel_id=1, source_target_pairs={{16,24},{17,25},{18,26},{19,27},{20,28},{21,29},{22,30},{23,31}} | collective-permute-start | bytes 786440 | tf_op jit(solution)/shard_map/ppermute | solution.py:293
  257.1 1.0 copy-start.4
  258.0 0.9 copy-start.7
  259.0 0.9 copy-start.10
  (3 other events, 2.4 us)
Sparse Core Ops, SparseCore 0:
  36.3 66.1 all-reduce.2
where the time goes:
time: 275 us; the launch traced here: 272 us
  waiting for transfers between devices  149 us (54%)
  Pallas kernels  49.7 us (18%)
  starting transfers between devices  33.3 us (12%)
  local copies, waits for them, and re-layouts  21.8 us (8%)
  between operations  13.7 us (5%)
  other arithmetic  4.6 us (2%)
    psum x1, waiting for transfers between devices, shards(): own_margins = [lax.psum(term, 'pw') for term in terms]  64.8 us
    ppermute x18, waiting for transfers between devices, other_chip(): lax.ppermute(block, 'pw', [(i, (i + 2 * distance) % size) for i in range(...  39.6 us
    pallas_call x4, Pallas kernels, margin_section(): pl.pallas_call(functools.partial(margin_kernel, steps, len(other_specs) /...  36.5 us
    ppermute x18, starting transfers between devices, other_chip(): lax.ppermute(block, 'pw', [(i, (i + 2 * distance) % size) for i in range(...  26.4 us
    ppermute x2, waiting for transfers between devices, shards(): starts.append([lax.ppermute(line, 'ka', [(number, number + 1)])])  20.7 us
    ppermute x3, waiting for transfers between devices, send(): lax.ppermute(after(blocks[number], earlier) if earlier else blocks[number...  18.5 us
    unnamed x36, local copies, waits for them, and re-layouts  16.5 us
    pallas_call x1, Pallas kernels, packed_now(): pl.pallas_call(pack_kernel, grid=(width // step,), in_specs=[pl.BlockSpec...  6.59 us
  transfers between devices with their start and end apart: 33, of which 21 were waited for; matrix products, arithmetic and copies ran while one was open for 3% of the time, Pallas kernels for 11%

commit v1 on v0

--- a/solution.py
+++ b/solution.py
@@ -79,11 +79,14 @@
         other_specs = [pl.BlockSpec((None, bands, depth), lambda step: (kpoint + 1, 0, step))] * 2
         others = states
     else:
-        widths = [other.shape[0] // 2 for other in others]
+        packs = [other if isinstance(other, tuple) else (other, other) for other in others]
+        apart = [isinstance(other, tuple) for other in others]
+        widths = [pack[0].shape[0] // (1 if one else 2) for pack, one in zip(packs, apart)]
         width = sum(widths)
         other_specs = [pl.BlockSpec((one, depth), lambda step: (0, step)) for one in widths]
-        other_specs += [pl.BlockSpec((one, depth), lambda step: (1, step)) for one in widths]
-        others = [*others, *others]
+        for one, alone in zip(widths, apart):
+            other_specs.append(pl.BlockSpec((one, depth), functools.partial(lambda row, step: (row, step), 0 if alone else 1)))
+        others = [pack[0] for pack in packs] + [pack[1] for pack in packs]
     operands, specs = [*states, *others], [own, own, *other_specs]
     if left is not None:
         operands += left
@@ -117,8 +120,9 @@
 def split(value):
     return pl.pallas_call(
         split_kernel,
+        out_specs=[pl.BlockSpec(memory_space=pltpu.VMEM)] * 2,
         out_shape=[jax.ShapeDtypeStruct(value.shape, jnp.bfloat16)] * 2,
-        compiler_params=pltpu.CompilerParams(vmem_limit_bytes=VMEM_LIMIT),
+        compiler_params=pltpu.CompilerParams(vmem_limit_bytes=12 * 1024 * 1024),
     )(value)
 
 
@@ -132,22 +136,30 @@
     return jnp.concatenate([jnp.concatenate(reals, 1), jnp.concatenate(imags, 1)], 0)
 
 
-def whole_piece(refs, place):
-    if refs[0].dtype == jnp.bfloat16:
-        return refs[0][...], refs[1][...]
-    if len(refs) == 1:
-        return halves_of(refs[0][...])
-    mine, theirs = refs
-    chips = mine.shape[0]
-    blocks = []
+def join_kernel(place, mine, theirs, high, low):
+    chips, rows, _ = mine.shape
     for chip in range(chips):
         turn = lax.rem(place[0] - chip + chips, chips)
         one, other = mine[turn], theirs[turn]
-        blocks += [jnp.where(place[1] == 0, one, other), jnp.where(place[1] == 0, other, one)]
-    return halves_of(jnp.concatenate(blocks, 0))
-
-
-def rows_kernel(tree, place, *refs):
+        for core in (0, 1):
+            block = jnp.where(place[1] == core, one, other)
+            where = pl.ds((2 * chip + core) * rows, rows)
+            high[where, :], low[where, :] = halves_of(block)
+
+
+def joined(place, mine, theirs):
+    chips, rows, columns = mine.shape
+    return pl.pallas_call(
+        join_kernel,
+        in_specs=[pl.BlockSpec(memory_space=pltpu.SMEM)] + [pl.BlockSpec((chips, rows, columns), lambda: (0, 0, 0))] * 2,
+        out_specs=[pl.BlockSpec(memory_space=pltpu.VMEM)] * 2,
+        out_shape=[jax.ShapeDtypeStruct((2 * chips * rows, columns), jnp.bfloat16)] * 2,
+        compiler_params=pltpu.CompilerParams(vmem_limit_bytes=12 * 1024 * 1024),
+        cost_estimate=pl.CostEstimate(flops=0, bytes_accessed=0, transcendentals=0),
+    )(place, mine, theirs)
+
+
+def rows_kernel(tree, *refs):
     out = refs[-1]
     terms, matrices = jax.tree.unflatten(tree, refs[:-1])
     flat = whole_rows(terms[0])
@@ -159,9 +171,8 @@
     for number, matrix in enumerate(matrices):
         first = 0
         for piece in matrix:
-            piece_high, piece_low = whole_piece(piece, place)
-            product = dot(both, piece_high)
-            product = product[: 2 * count] + product[2 * count :] + dot(high, piece_low)
+            product = dot(both, piece[0][...])
+            product = product[: 2 * count] + product[2 * count :] + dot(high, piece[1][...])
             width = product.shape[1] // 2
             columns = slice(first, first + width)
             out[number, 0, :, columns] = product[:count, :width] - product[count:, width:]
@@ -169,33 +180,16 @@
             first += width
 
 
-def rows_times(place, terms, matrices, count, bands):
+def rows_times(terms, matrices, count, bands):
     flat, tree = jax.tree.flatten((terms, matrices))
+    in_vmem = pl.BlockSpec(memory_space=pltpu.VMEM)
     return pl.pallas_call(
         functools.partial(rows_kernel, tree),
-        in_specs=[pl.BlockSpec(memory_space=pltpu.SMEM)] + [pl.BlockSpec(memory_space=pltpu.VMEM)] * len(flat),
+        in_specs=[in_vmem if one.dtype == jnp.bfloat16 else pl.BlockSpec() for one in flat],
         out_shape=jax.ShapeDtypeStruct((len(matrices), 2, count, bands), jnp.float32),
-        compiler_params=pltpu.CompilerParams(vmem_limit_bytes=24 * 1024 * 1024),
+        compiler_params=pltpu.CompilerParams(vmem_limit_bytes=12 * 1024 * 1024),
         cost_estimate=pl.CostEstimate(flops=0, bytes_accessed=0, transcendentals=0),
-    )(place, *flat)
-
-
-def pack_kernel(re_ref, im_ref, out):
-    out[0] = re_ref[...]
-    out[1] = im_ref[...]
-
-
-def packed_now(states, kpoint, width):
-    waves = states[0].shape[2]
-    step = min(32, width)
-    return pl.pallas_call(
-        pack_kernel,
-        grid=(width // step,),
-        in_specs=[pl.BlockSpec((None, step, waves), lambda i: (kpoint, i, 0))] * 2,
-        out_specs=pl.BlockSpec((2, step, waves), lambda i: (0, i, 0)),
-        out_shape=jax.ShapeDtypeStruct((2, width, waves), states[0].dtype),
-        compiler_params=pltpu.CompilerParams(vmem_limit_bytes=60 * 1024 * 1024),
-    )(*states).reshape(2 * width, waves)
+    )(*flat)
 
 
 def packed(states, kpoint, first, width):
@@ -246,7 +240,7 @@
     widths = [2 * quarter, quarter, quarter]
     firsts = [sum(widths[:i]) for i in range(len(widths))]
     to_previous = [(i, (i - 1) % ka_width) for i in range(ka_width)]
-    blocks = [packed_now((states_re, states_im), 0, widths[0])]
+    blocks = [tuple(state[0, : widths[0]] for state in (states_re, states_im))]
     blocks += [packed((states_re, states_im), 0, first, width) for first, width in zip(firsts[1:], widths[1:])]
 
     def send(number, *earlier):
@@ -261,40 +255,42 @@
     before = own_margins[0]
     for k in range(1, last):
         rows = jnp.stack([before[:, :bands], before[:, bands:]], 0)
-        before = rows_times(place, [[rows]], [[[own_margins[k]]]], bands, bands)[0]
+        before = rows_times([[rows]], [[split(own_margins[k])]], bands, bands)[0]
         before = jnp.concatenate([before[0], before[1]], 1)
         own_margins[k] = before
     left = split(after(before, arrivals[0]))
 
     rows, span = [], []
+    half = ready = None
     for number in range(len(widths)):
         piece = arrivals[number]
-        if number > 0:
+        final = number == len(widths) - 1
+        if final:
+            reals = [one[:, : one.shape[1] // 2] for one in rows]
+            imags = [one[:, one.shape[1] // 2 :] for one in rows]
+            ready = lax.ppermute(after(jnp.concatenate(reals + imags, 1), (piece, span)), "ka", [(0, 1)])
+        if half is not None:
             piece = after(piece, half)
         mine, theirs = margin_section(states, last, [piece], left, core)
         if number == 0:
             arrivals.append(send(2, arrivals[0], mine))
-        rows.append(sum_to_rows(mine, theirs))
-        if number == len(widths) - 1:
-            ready = lax.ppermute(after(tuple(rows[:-1]), piece), "ka", [(0, 1)])
-            half = rows_to_core(after(rows[-1], ready))
-            received = [*ready, lax.ppermute(rows[-1], "ka", [(0, 1)])]
-            half_ready = after(half, received[-1])
-        else:
-            half = half_ready = rows_to_core(rows[-1])
-        span.append([half_ready, other_core(half_ready)])
+        rows.append(sum_to_rows(mine, after(theirs, ready) if final else theirs))
+        half = rows_to_core(rows[-1])
+        if final:
+            received = [ready, lax.ppermute(rows[-1], "ka", [(0, 1)])]
+            half = after(half, received[-1])
+        span.append(joined(place, half, other_core(half)))
 
     row_index = lax.broadcasted_iota(jnp.int32, (band_rows, bands), 0) + first_band
     col_index = lax.broadcasted_iota(jnp.int32, (band_rows, bands), 1)
     eye_real = jnp.where((row_index == col_index) & (ka_place == 0), 1.0, 0.0).astype(jnp.float32)
     starts = [[jnp.stack([eye_real, jnp.zeros_like(eye_real)], 0)], received]
     for number in range(1, ka_width - 1):
-        line = rows_times(place, starts[-1:], [span], band_rows, bands)[0]
+        line = rows_times(starts[-1:], [span], band_rows, bands)[0]
         starts.append([lax.ppermute(line, "ka", [(number, number + 1)])])
 
-    margins = [[[margin]] for margin in own_margins]
-    margins[-1] = [left]
-    lines = rows_times(place, starts, margins + [span], band_rows, bands)
+    margins = [[split(margin)] for margin in own_margins[:-1]] + [[left]]
+    lines = rows_times(starts, margins + [span], band_rows, bands)
     return jnp.moveaxis(lines, 1, 2)
 
 

time: 275 us -> 264 us (0.960); the launches traced: 272 us -> 264 us
  waiting for transfers between devices: 149 us -> 140 us
  Pallas kernels: 49.7 us -> 43.8 us
  local copies, waits for them, and re-layouts: 21.8 us -> 27.5 us
    ppermute x3 -> x4, waiting for transfers between devices: 18.5 us -> 11.1 us  [send(): lax.ppermute(after(blocks[number], earlier) if earlier else blocks[number...]
    squeeze x0 -> x2, local copies, waits for them, and re-layouts: none -> 6.48 us  [shards(): blocks = [tuple((state[0, :widths[0]] for state in (states_re, states_im)))]]
    pallas_call x5 -> x7, Pallas kernels: 13.2 us -> 7.82 us  [the longest x3 5.52 us: rows_times(): pl.pallas_call(functools.partial(rows_kernel, tree), in_specs=[in_vmem if...]
    ppermute x2, waiting for transfers between devices: 20.7 us -> 16.8 us  [shards(): starts.append([lax.ppermute(line, 'ka', [(number, number + 1)])])]
    unnamed x36 -> x32, local copies, waits for them, and re-layouts: 16.5 us -> 14.2 us
  transfers between devices with their start and end apart: 33 -> 33, of which waited for: 21 -> 20; matrix products, arithmetic and copies ran while one was open for 3% -> 6% of each run, Pallas kernels for 11% -> 14%
where the time goes in v1:
time: 264 us
  waiting for transfers between devices  140 us (53%)
  Pallas kernels  43.8 us (17%)
  starting transfers between devices  31.9 us (12%)
  local copies, waits for them, and re-layouts  27.5 us (10%)
  between operations  13.8 us (5%)
  other arithmetic  6.16 us (2%)
    psum x1, waiting for transfers between devices, shards(): own_margins = [lax.psum(term, 'pw') for term in terms]  66 us
    ppermute x18, waiting for transfers between devices, other_chip(): lax.ppermute(block, 'pw', [(i, (i + 2 * distance) % size) for i in range(...  41.2 us
    pallas_call x4, Pallas kernels, margin_section(): pl.pallas_call(functools.partial(margin_kernel, steps, len(other_specs) /...  36 us
    ppermute x18, starting transfers between devices, other_chip(): lax.ppermute(block, 'pw', [(i, (i + 2 * distance) % size) for i in range(...  24.9 us
    ppermute x2, waiting for transfers between devices, shards(): starts.append([lax.ppermute(line, 'ka', [(number, number + 1)])])  16.8 us
    unnamed x32, local copies, waits for them, and re-layouts  14.2 us
    ppermute x4, waiting for transfers between devices, send(): lax.ppermute(after(blocks[number], earlier) if earlier else blocks[number...  11.1 us
    squeeze x2, local copies, waits for them, and re-layouts, shards(): blocks = [tuple((state[0, :widths[0]] for state in (states_re, states_im)))]  6.48 us
  transfers between devices with their start and end apart: 33, of which 20 were waited for; matrix products, arithmetic and copies ran while one was open for 6% of the time, Pallas kernels for 14%

profile of v1, /device:TPU:6, one launch (start us, length us, event | category | flops | bytes accessed | tf_op | source)
XLA Modules:
  0.0 263.6 jit_solution(12607489599502224906)
XLA Ops:
  6.5 3.3 %slice_bitcast_fusion.1 = bf16[256,4096]{1,0:T(8,128)(2,1)} fusion(bf16[2,512,4096]{2,1,0:T(8,128)(2,1)} %refs_1_.3), kind=kLoop, calls=%fused_computation.3 | loop fusion | bytes 4194304 | tf_op jit(solution)/shard_map/squeeze | solution.py:243
  10.4 3.2 %slice_bitcast_fusion = bf16[256,4096]{1,0:T(8,128)(2,1)} fusion(bf16[2,512,4096]{2,1,0:T(8,128)(2,1)} %refs_2_.3), kind=kLoop, calls=%fused_computation.2 | loop fusion | bytes 4194304 | tf_op jit(solution)/shard_map/squeeze | solution.py:243
  13.6 1.4 collective-permute-start.1
  15.0 2.7 %slice_bitcast_fusion.2 = (bf16[128,4096]{1,0:T(8,128)(2,1)}, bf16[128,4096]{1,0:T(8,128)(2,1)S(1)}) fusion(bf16[2,512,4096]{2,1,0:T(8,128)(2,1)} %refs_2_.3), kind=kLoop, calls=%fused_computation.4 | loop fusion | bytes 4194304 | tf_op jit(solution)/shard_map/squeeze | solution.py:196
  17.7 13.6 %shard_map.28 = f32[512,1024]{1,0:T(8,128)} custom-call(bf16[2,512,4096]{2,1,0:T(8,128)(2,1)S(1)} %copy-done, bf16[2,512,4096]{2,1,0:T(8,128)(2,1)} %refs_2_.3, bf16[2,512,4096]{2,1,0:T(8,128)(2,1)S(1)} %copy-done, bf16[2,512,4096]{2,1,0:T(8,128)(2,1)} %refs_2_.3), custom_call_target="tpu_custom_call" | custom-call | tf_op jit(solution)/shard_map/pallas_call | solution.py:104
  31.3 2.8 %slice_bitcast_fusion.3 = (bf16[128,4096]{1,0:T(8,128)(2,1)}, bf16[128,4096]{1,0:T(8,128)(2,1)S(1)}) fusion(bf16[2,512,4096]{2,1,0:T(8,128)(2,1)} %refs_1_.3), kind=kLoop, calls=%fused_computation.5 | loop fusion | bytes 4194304 | tf_op jit(solution)/shard_map/squeeze | solution.py:196
  34.1 1.5 pad_maximum_fusion
  36.2 66.0 %all-reduce.3.cloned.1.call-done.value = f32[512,1024]{1,0:T(8,128)} async-done(((f32[512,1024]{1,0:T(8,128)}), f32[512,1024]{1,0:T(8,128)}) %all-reduce.3.cloned.1.call-update) | async-done | bytes 2097168 | tf_op jit(solution)/shard_map/psum | solution.py:254
  102.1 1.3 copy-done.11
  104.5 1.6 copy-done.13
  106.4 1.3 copy-done.12
  107.7 9.5 %shard_map.30 = (f32[4,64,512]{2,1,0:T(8,128)S(1)}, f32[4,64,512]{2,1,0:T(8,128)S(1)}) custom-call(s32[1]{0:T(128)} %bitcast.refs_0_, bf16[2,512,4096]{2,1,0:T(8,128)(2,1)} %refs_1_.3, bf16[2,512,4096]{2,1,0:T(8,128)(2,1)} %refs_2_.3, bf16[256,4096]{1,0:T(8,128)(2,1)S(1)} %copy-done.12, bf16[256,4096]{1,0:T(8,128)(2,1)} %collective-permute-done.1.refs_4_, ...), custom_call_target="tpu_custom_call" | custom-call | tf_op jit(solution)/shard_map/pallas_call | solution.py:104
  117.3 3.1 %pad_maximum_fusion.1 = bf16[256,4096]{1,0:T(8,128)(2,1)} fusion(bf16[128,4096]{1,0:T(8,128)(2,1)} %get-tuple-element.55, bf16[128,4096]{1,0:T(8,128)(2,1)} %get-tuple-element.53), kind=kLoop, calls=%fused_computation.1 | loop fusion | flops 4194304 | bytes 4194304 | tf_op jit(solution)/shard_map/concatenate | solution.py:196
  120.4 1.1 add.113
  121.6 3.7 %collective-permute-start.5 = (f32[64,512]{1,0:T(8,128)S(1)}, f32[64,512]{1,0:T(8,128)S(1)}, u32[]{:S(2)}, u32[]{:S(2)}) collective-permute-start(f32[64,512]{1,0:T(8,128)S(1)} %get-tuple-element.58), channel_id=1, source_target_pairs={{0,6},{1,7},{2,0},{3,1},{4,2},{5,3},{6,4},{7,5},{8,14},{9,15},{10,... | collective-permute-start | bytes 393224 | tf_op jit(solution)/shard_map/ppermute | solution.py:210
  126.3 2.9 %collective-permute-done.5 = f32[64,512]{1,0:T(8,128)S(1)} collective-permute-done((f32[64,512]{1,0:T(8,128)S(1)}, f32[64,512]{1,0:T(8,128)S(1)}, u32[]{:S(2)}, u32[]{:S(2)}) %collective-permute-start.5) | collective-permute-done | bytes 131104 | tf_op jit(solution)/shard_map/ppermute | solution.py:210
  129.2 8.2 %collective-permute-done.4 = f32[64,512]{1,0:T(8,128)S(1)} collective-permute-done((f32[64,512]{1,0:T(8,128)S(1)}, f32[64,512]{1,0:T(8,128)S(1)}, u32[]{:S(2)}, u32[]{:S(2)}) %collective-permute-start.4) | collective-permute-done | bytes 131104 | tf_op jit(solution)/shard_map/ppermute | solution.py:210
  137.4 1.3 collective-permute-start.9
  138.7 1.2 collective-permute-start.8
  139.9 1.9 collective-permute-start.7
  141.9 1.3 collective-permute-done.9
  143.2 8.2 %collective-permute-done.8 = f32[64,512]{1,0:T(8,128)S(1)} collective-permute-done((f32[64,512]{1,0:T(8,128)S(1)}, f32[64,512]{1,0:T(8,128)S(1)}, u32[]{:S(2)}, u32[]{:S(2)}) %collective-permute-start.8) | collective-permute-done | bytes 131104 | tf_op jit(solution)/shard_map/ppermute | solution.py:210
  151.4 3.4 %copy-done.1 = bf16[2,512,4096]{2,1,0:T(8,128)(2,1)S(1)} copy-done((bf16[2,512,4096]{2,1,0:T(8,128)(2,1)S(1)}, bf16[2,512,4096]{2,1,0:T(8,128)(2,1)}, u32[]{:S(2)}) %copy-start.1) | copy-done | bytes 8388632
  154.8 6.5 %shard_map.31 = (f32[4,64,256]{2,1,0:T(8,128)S(1)}, f32[4,64,256]{2,1,0:T(8,128)S(1)}) custom-call(s32[1]{0:T(128)} %bitcast.refs_0_, bf16[2,512,4096]{2,1,0:T(8,128)(2,1)S(1)} %copy-done.1, bf16[2,512,4096]{2,1,0:T(8,128)(2,1)} %refs_2_.3, bf16[256,4096]{1,0:T(8,128)(2,1)} %collective-permute-done.6.refs_3_.refs_4_, ...), custom_call_target="tpu_custom_call" | custom-call | tf_op jit(solution)/shard_map/pallas_call | solution.py:104
  161.4 1.5 collective-permute-done.10
  162.9 1.7 collective-permute-start.13
  164.6 1.7 collective-permute-start.11
  167.3 4.8 %collective-permute-done.12 = f32[64,256]{1,0:T(8,128)S(1)} collective-permute-done((f32[64,256]{1,0:T(8,128)S(1)}, f32[64,256]{1,0:T(8,128)S(1)}, u32[]{:S(2)}, u32[]{:S(2)}) %collective-permute-start.12) | collective-permute-done | bytes 65568 | tf_op jit(solution)/shard_map/ppermute | solution.py:210
  172.1 1.4 collective-permute-start.18
  174.0 1.9 collective-permute-start.16
  176.4 4.5 %collective-permute-done.17 = f32[64,256]{1,0:T(8,128)S(1)} collective-permute-done((f32[64,256]{1,0:T(8,128)S(1)}, f32[64,256]{1,0:T(8,128)S(1)}, u32[]{:S(2)}, u32[]{:S(2)}) %collective-permute-start.17) | collective-permute-done | bytes 65568 | tf_op jit(solution)/shard_map/ppermute | solution.py:210
  183.2 10.0 %collective-permute-done.14.refs_3_.refs_4_ = bf16[256,4096]{1,0:T(8,128)(2,1)} collective-permute-done((bf16[256,4096]{1,0:T(8,128)(2,1)}, bf16[256,4096]{1,0:T(8,128)(2,1)}, u32[]{:S(2)}, u32[]{:S(2)}) %collective-permute-start.14) | collective-permute-done | bytes 2097184 | tf_op jit(solution)/shard_map/ppermute | solution.py:247
  194.1 6.5 %shard_map.34 = (f32[4,64,256]{2,1,0:T(8,128)S(1)}, f32[4,64,256]{2,1,0:T(8,128)S(1)}) custom-call(s32[1]{0:T(128)} %bitcast.refs_0_, bf16[2,512,4096]{2,1,0:T(8,128)(2,1)S(1)} %copy-done.1, bf16[2,512,4096]{2,1,0:T(8,128)(2,1)} %refs_2_.3, bf16[256,4096]{1,0:T(8,128)(2,1)} %collective-permute-done.14.refs_3_.refs_4_, ...), custom_call_target="tpu_custom_call" | custom-call | tf_op jit(solution)/shard_map/pallas_call | solution.py:104
  200.7 1.5 collective-permute-done.21
  202.3 3.6 %collective-permute-start.24 = (f32[64,256]{1,0:T(8,128)S(1)}, f32[64,256]{1,0:T(8,128)S(1)}, u32[]{:S(2)}, u32[]{:S(2)}) collective-permute-start(f32[64,256]{1,0:T(8,128)S(1)} %get-tuple-element.61), channel_id=1, source_target_pairs={{0,6},{1,7},{2,0},{3,1},{4,2},{5,3},{6,4},{7,5},{8,14},{9,15},{10,... | collective-permute-start | bytes 196616 | tf_op jit(solution)/shard_map/ppermute | solution.py:210
  206.9 1.4 collective-permute-done.24
  208.4 4.3 %collective-permute-done.23 = f32[64,256]{1,0:T(8,128)S(1)} collective-permute-done((f32[64,256]{1,0:T(8,128)S(1)}, f32[64,256]{1,0:T(8,128)S(1)}, u32[]{:S(2)}, u32[]{:S(2)}) %collective-permute-start.23) | collective-permute-done | bytes 65568 | tf_op jit(solution)/shard_map/ppermute | solution.py:210
  212.7 1.9 collective-permute-start.28
  214.6 1.9 collective-permute-start.26
  217.6 3.9 %collective-permute-done.27 = f32[64,256]{1,0:T(8,128)S(1)} collective-permute-done((f32[64,256]{1,0:T(8,128)S(1)}, f32[64,256]{1,0:T(8,128)S(1)}, u32[]{:S(2)}, u32[]{:S(2)}) %collective-permute-start.27) | collective-permute-done | bytes 65568 | tf_op jit(solution)/shard_map/ppermute | solution.py:210
  221.6 1.5 collective-permute-done.29.theirs
  223.8 1.3 shard_map.36
  225.1 1.4 collective-permute-start.30
  229.3 2.2 shard_map.37
  231.6 1.3 collective-permute-start.31
  233.0 16.8 %collective-permute-done.31.refs_4_ = f32[2,64,512]{2,1,0:T(8,128)} collective-permute-done((f32[2,64,512]{2,1,0:T(8,128)}, f32[2,64,512]{2,1,0:T(8,128)}, u32[]{:S(2)}, u32[]{:S(2)}) %collective-permute-start.31) | collective-permute-done | bytes 262176 | tf_op jit(solution)/shard_map/ppermute | solution.py:290
  253.5 2.0 shard_map.38
  255.6 1.2 copy.3
  (88 shorter events, 18.4 us)
Async XLA Ops:
  6.5 95.6 %all-reduce.3.cloned.1.call-start = ((), (), s32[]{:S(2)}) async-start(), calls=%async_computation | async-start | bytes 4194304 | tf_op jit(solution)/shard_map/psum | solution.py:254
  6.5 11.2 %copy-start = (bf16[2,512,4096]{2,1,0:T(8,128)(2,1)S(1)}, bf16[2,512,4096]{2,1,0:T(8,128)(2,1)}, u32[]{:S(2)}) copy-start(bf16[2,512,4096]{2,1,0:T(8,128)(2,1)} %refs_1_.3) | copy-start | bytes 25165828
  9.8 92.3 %collective-permute-start = (bf16[256,4096]{1,0:T(8,128)(2,1)}, bf16[256,4096]{1,0:T(8,128)(2,1)S(1)}, u32[]{:S(2)}, u32[]{:S(2)}) collective-permute-start(bf16[256,4096]{1,0:T(8,128)(2,1)} %slice_bitcast_fusion.1), channel_id=1, source_target_pairs={{0,24},{8,0},{16,8},{24,16},{1,25},{9,1},{17,9},{25,17},{2,26},{10... | collective-permute-start | bytes 6291464 | tf_op jit(solution)/shard_map/ppermute | solution.py:247
  13.6 90.9 %collective-permute-start.1 = (bf16[256,4096]{1,0:T(8,128)(2,1)}, bf16[256,4096]{1,0:T(8,128)(2,1)}, u32[]{:S(2)}, u32[]{:S(2)}) collective-permute-start(bf16[256,4096]{1,0:T(8,128)(2,1)} %slice_bitcast_fusion), channel_id=1, source_target_pairs={{0,24},{8,0},{16,8},{24,16},{1,25},{9,1},{17,9},{25,17},{2,26},{10... | collective-permute-start | bytes 6291464 | tf_op jit(solution)/shard_map/ppermute | solution.py:247
  35.6 115.8 %collective-permute-start.6 = (bf16[256,4096]{1,0:T(8,128)(2,1)}, bf16[256,4096]{1,0:T(8,128)(2,1)}, u32[]{:S(2)}, u32[]{:S(2)}) collective-permute-start(bf16[256,4096]{1,0:T(8,128)(2,1)} %pad_maximum_fusion), channel_id=1, source_target_pairs={{0,24},{8,0},{16,8},{24,16},{1,25},{9,1},{17,9},{25,17},{2,26},{10... | collective-permute-start | bytes 6291464 | tf_op jit(solution)/shard_map/ppermute | solution.py:247
  102.1 1.3 copy-start.11
  104.5 1.6 copy-start.13
  106.1 1.6 copy-start.12
  117.2 3.3 %collective-permute-start.2 = (f32[4,64,512]{2,1,0:T(8,128)S(1)}, f32[4,64,512]{2,1,0:T(8,128)}, u32[]{:S(2)}, u32[]{:S(2)}) collective-permute-start(f32[4,64,512]{2,1,0:T(8,128)S(1)} %get-tuple-element.35), channel_id=1, source_target_pairs={{0,1},{1,0},{2,3},{3,2},{4,5},{5,4},{6,7},{7,6},{8,9},{9,8},{10,11... | collective-permute-start | bytes 1572872 | tf_op jit(solution)/shard_map/ppermute | solution.py:205
  120.4 72.8 %collective-permute-start.14 = (bf16[256,4096]{1,0:T(8,128)(2,1)}, bf16[256,4096]{1,0:T(8,128)(2,1)}, u32[]{:S(2)}, u32[]{:S(2)}) collective-permute-start(bf16[256,4096]{1,0:T(8,128)(2,1)} %pad_maximum_fusion.1), channel_id=1, source_target_pairs={{0,24},{8,0},{16,8},{24,16},{1,25},{9,1},{17,9},{25,17},{2,26},{10... | collective-permute-start | bytes 6291464 | tf_op jit(solution)/shard_map/ppermute | solution.py:247
  121.6 7.6 %collective-permute-start.5 = (f32[64,512]{1,0:T(8,128)S(1)}, f32[64,512]{1,0:T(8,128)S(1)}, u32[]{:S(2)}, u32[]{:S(2)}) collective-permute-start(f32[64,512]{1,0:T(8,128)S(1)} %get-tuple-element.58), channel_id=1, source_target_pairs={{0,6},{1,7},{2,0},{3,1},{4,2},{5,3},{6,4},{7,5},{8,14},{9,15},{10,... | collective-permute-start | bytes 393224 | tf_op jit(solution)/shard_map/ppermute | solution.py:210
  125.3 12.1 %collective-permute-start.4 = (f32[64,512]{1,0:T(8,128)S(1)}, f32[64,512]{1,0:T(8,128)S(1)}, u32[]{:S(2)}, u32[]{:S(2)}) collective-permute-start(f32[64,512]{1,0:T(8,128)S(1)} %get-tuple-element.59), channel_id=1, source_target_pairs={{0,4},{1,5},{2,6},{3,7},{4,0},{5,1},{6,2},{7,3},{8,12},{9,13},{10,... | collective-permute-start | bytes 393224 | tf_op jit(solution)/shard_map/ppermute | solution.py:210
  125.3 12.1 %collective-permute-start.3 = (f32[64,512]{1,0:T(8,128)S(1)}, f32[64,512]{1,0:T(8,128)S(1)}, u32[]{:S(2)}, u32[]{:S(2)}) collective-permute-start(f32[64,512]{1,0:T(8,128)S(1)} %get-tuple-element.57), channel_id=1, source_target_pairs={{0,2},{1,3},{2,4},{3,5},{4,6},{5,7},{6,0},{7,1},{8,10},{9,11},{10,... | collective-permute-start | bytes 393224 | tf_op jit(solution)/shard_map/ppermute | solution.py:210
  137.4 5.8 %collective-permute-start.9 = (f32[64,512]{1,0:T(8,128)S(1)}, f32[64,512]{1,0:T(8,128)S(1)}, u32[]{:S(2)}, u32[]{:S(2)}) collective-permute-start(f32[64,512]{1,0:T(8,128)S(1)} %fusion.1), channel_id=1, source_target_pairs={{0,6},{1,7},{2,0},{3,1},{4,2},{5,3},{6,4},{7,5},{8,14},{9,15},{10,... | collective-permute-start | bytes 393224 | tf_op jit(solution)/shard_map/ppermute | solution.py:210
  138.7 12.7 %collective-permute-start.8 = (f32[64,512]{1,0:T(8,128)S(1)}, f32[64,512]{1,0:T(8,128)S(1)}, u32[]{:S(2)}, u32[]{:S(2)}) collective-permute-start(f32[64,512]{1,0:T(8,128)S(1)} %fusion.1), channel_id=1, source_target_pairs={{0,4},{1,5},{2,6},{3,7},{4,0},{5,1},{6,2},{7,3},{8,12},{9,13},{10,... | collective-permute-start | bytes 393224 | tf_op jit(solution)/shard_map/ppermute | solution.py:210
  139.9 11.5 %collective-permute-start.7 = (f32[64,512]{1,0:T(8,128)S(1)}, f32[64,512]{1,0:T(8,128)S(1)}, u32[]{:S(2)}, u32[]{:S(2)}) collective-permute-start(f32[64,512]{1,0:T(8,128)S(1)} %fusion.1), channel_id=1, source_target_pairs={{0,2},{1,3},{2,4},{3,5},{4,6},{5,7},{6,0},{7,1},{8,10},{9,11},{10,... | collective-permute-start | bytes 393224 | tf_op jit(solution)/shard_map/ppermute | solution.py:210
  151.4 3.4 %copy-start.1 = (bf16[2,512,4096]{2,1,0:T(8,128)(2,1)S(1)}, bf16[2,512,4096]{2,1,0:T(8,128)(2,1)}, u32[]{:S(2)}) copy-start(bf16[2,512,4096]{2,1,0:T(8,128)(2,1)} %refs_1_.3) | copy-start | bytes 25165828
  161.3 1.6 collective-permute-start.10
  162.9 4.3 %collective-permute-start.13 = (f32[64,256]{1,0:T(8,128)S(1)}, f32[64,256]{1,0:T(8,128)S(1)}, u32[]{:S(2)}, u32[]{:S(2)}) collective-permute-start(f32[64,256]{1,0:T(8,128)S(1)} %get-tuple-element.64), channel_id=1, source_target_pairs={{0,6},{1,7},{2,0},{3,1},{4,2},{5,3},{6,4},{7,5},{8,14},{9,15},{10,... | collective-permute-start | bytes 196616 | tf_op jit(solution)/shard_map/ppermute | solution.py:210
  164.6 7.5 %collective-permute-start.12 = (f32[64,256]{1,0:T(8,128)S(1)}, f32[64,256]{1,0:T(8,128)S(1)}, u32[]{:S(2)}, u32[]{:S(2)}) collective-permute-start(f32[64,256]{1,0:T(8,128)S(1)} %get-tuple-element.65), channel_id=1, source_target_pairs={{0,4},{1,5},{2,6},{3,7},{4,0},{5,1},{6,2},{7,3},{8,12},{9,13},{10,... | collective-permute-start | bytes 196616 | tf_op jit(solution)/shard_map/ppermute | solution.py:210
  164.6 7.5 %collective-permute-start.11 = (f32[64,256]{1,0:T(8,128)S(1)}, f32[64,256]{1,0:T(8,128)S(1)}, u32[]{:S(2)}, u32[]{:S(2)}) collective-permute-start(f32[64,256]{1,0:T(8,128)S(1)} %get-tuple-element.63), channel_id=1, source_target_pairs={{0,2},{1,3},{2,4},{3,5},{4,6},{5,7},{6,0},{7,1},{8,10},{9,11},{10,... | collective-permute-start | bytes 196616 | tf_op jit(solution)/shard_map/ppermute | solution.py:210
  166.4 14.7 %collective-permute-start.15 = (f32[4,64,512]{2,1,0:T(8,128)S(1)}, f32[4,64,512]{2,1,0:T(8,128)S(1)}, u32[]{:S(2)}, u32[]{:S(2)}) collective-permute-start(f32[4,64,512]{2,1,0:T(8,128)S(1)} %pad_maximum_fusion.2.mine), channel_id=1, source_target_pairs={{0,1},{1,0},{2,3},{3,2},{4,5},{5,4},{6,7},{7,6},{8,9},{9,8},{10,11... | collective-permute-start | bytes 1572872 | tf_op jit(solution)/shard_map/ppermute | solution.py:205
  172.1 4.3 %collective-permute-start.18 = (f32[64,256]{1,0:T(8,128)S(1)}, f32[64,256]{1,0:T(8,128)S(1)}, u32[]{:S(2)}, u32[]{:S(2)}) collective-permute-start(f32[64,256]{1,0:T(8,128)S(1)} %fusion.7), channel_id=1, source_target_pairs={{0,6},{1,7},{2,0},{3,1},{4,2},{5,3},{6,4},{7,5},{8,14},{9,15},{10,... | collective-permute-start | bytes 196616 | tf_op jit(solution)/shard_map/ppermute | solution.py:210
  173.5 7.4 %collective-permute-start.17 = (f32[64,256]{1,0:T(8,128)S(1)}, f32[64,256]{1,0:T(8,128)S(1)}, u32[]{:S(2)}, u32[]{:S(2)}) collective-permute-start(f32[64,256]{1,0:T(8,128)S(1)} %fusion.7), channel_id=1, source_target_pairs={{0,4},{1,5},{2,6},{3,7},{4,0},{5,1},{6,2},{7,3},{8,12},{9,13},{10,... | collective-permute-start | bytes 196616 | tf_op jit(solution)/shard_map/ppermute | solution.py:210
  174.0 7.0 %collective-permute-start.16 = (f32[64,256]{1,0:T(8,128)S(1)}, f32[64,256]{1,0:T(8,128)S(1)}, u32[]{:S(2)}, u32[]{:S(2)}) collective-permute-start(f32[64,256]{1,0:T(8,128)S(1)} %fusion.7), channel_id=1, source_target_pairs={{0,2},{1,3},{2,4},{3,5},{4,6},{5,7},{6,0},{7,1},{8,10},{9,11},{10,... | collective-permute-start | bytes 196616 | tf_op jit(solution)/shard_map/ppermute | solution.py:210
  181.0 1.6 collective-permute-start.19
  183.2 40.6 %copy-start.2 = (bf16[512,256]{1,0:T(8,128)(2,1)}, bf16[512,256]{1,0:T(8,128)(2,1)S(1)}, u32[]{:S(2)}) copy-start(bf16[512,256]{1,0:T(8,128)(2,1)S(1)} %get-tuple-element.44.refs_5_.refs_4_.refs_10_) | copy-start | bytes 786436
  193.2 7.4 %collective-permute-start.20 = (f32[64,768]{1,0:T(8,128)S(1)}, f32[64,768]{1,0:T(8,128)S(1)}, u32[]{:S(2)}, u32[]{:S(2)}) collective-permute-start(f32[64,768]{1,0:T(8,128)S(1)} %pad_maximum_fusion.5), channel_id=1, source_target_pairs={{0,8},{1,9},{2,10},{3,11},{4,12},{5,13},{6,14},{7,15}} | collective-permute-start | bytes 589832 | tf_op jit(solution)/shard_map/ppermute | solution.py:271
  200.6 24.5 %copy-start.14 = (f32[64,768]{1,0:T(8,128)}, f32[64,768]{1,0:T(8,128)S(1)}, u32[]{:S(2)}) copy-start(f32[64,768]{1,0:T(8,128)S(1)} %collective-permute-done.20.refs_0_.refs_1_) | copy-start | bytes 589828
  200.6 1.6 collective-permute-start.21
  202.3 6.1 %collective-permute-start.24 = (f32[64,256]{1,0:T(8,128)S(1)}, f32[64,256]{1,0:T(8,128)S(1)}, u32[]{:S(2)}, u32[]{:S(2)}) collective-permute-start(f32[64,256]{1,0:T(8,128)S(1)} %get-tuple-element.61), channel_id=1, source_target_pairs={{0,6},{1,7},{2,0},{3,1},{4,2},{5,3},{6,4},{7,5},{8,14},{9,15},{10,... | collective-permute-start | bytes 196616 | tf_op jit(solution)/shard_map/ppermute | solution.py:210
  205.9 6.8 %collective-permute-start.23 = (f32[64,256]{1,0:T(8,128)S(1)}, f32[64,256]{1,0:T(8,128)S(1)}, u32[]{:S(2)}, u32[]{:S(2)}) collective-permute-start(f32[64,256]{1,0:T(8,128)S(1)} %get-tuple-element.62), channel_id=1, source_target_pairs={{0,4},{1,5},{2,6},{3,7},{4,0},{5,1},{6,2},{7,3},{8,12},{9,13},{10,... | collective-permute-start | bytes 196616 | tf_op jit(solution)/shard_map/ppermute | solution.py:210
  205.9 6.8 %collective-permute-start.22 = (f32[64,256]{1,0:T(8,128)S(1)}, f32[64,256]{1,0:T(8,128)S(1)}, u32[]{:S(2)}, u32[]{:S(2)}) collective-permute-start(f32[64,256]{1,0:T(8,128)S(1)} %get-tuple-element.60), channel_id=1, source_target_pairs={{0,2},{1,3},{2,4},{3,5},{4,6},{5,7},{6,0},{7,1},{8,10},{9,11},{10,... | collective-permute-start | bytes 196616 | tf_op jit(solution)/shard_map/ppermute | solution.py:210
  212.7 4.9 %collective-permute-start.28 = (f32[64,256]{1,0:T(8,128)S(1)}, f32[64,256]{1,0:T(8,128)S(1)}, u32[]{:S(2)}, u32[]{:S(2)}) collective-permute-start(f32[64,256]{1,0:T(8,128)S(1)} %fusion.5), channel_id=1, source_target_pairs={{0,6},{1,7},{2,0},{3,1},{4,2},{5,3},{6,4},{7,5},{8,14},{9,15},{10,... | collective-permute-start | bytes 196616 | tf_op jit(solution)/shard_map/ppermute | solution.py:210
  214.6 6.9 %collective-permute-start.27 = (f32[64,256]{1,0:T(8,128)S(1)}, f32[64,256]{1,0:T(8,128)S(1)}, u32[]{:S(2)}, u32[]{:S(2)}) collective-permute-start(f32[64,256]{1,0:T(8,128)S(1)} %fusion.5), channel_id=1, source_target_pairs={{0,4},{1,5},{2,6},{3,7},{4,0},{5,1},{6,2},{7,3},{8,12},{9,13},{10,... | collective-permute-start | bytes 196616 | tf_op jit(solution)/shard_map/ppermute | solution.py:210
  214.6 6.9 %collective-permute-start.26 = (f32[64,256]{1,0:T(8,128)S(1)}, f32[64,256]{1,0:T(8,128)S(1)}, u32[]{:S(2)}, u32[]{:S(2)}) collective-permute-start(f32[64,256]{1,0:T(8,128)S(1)} %fusion.5), channel_id=1, source_target_pairs={{0,2},{1,3},{2,4},{3,5},{4,6},{5,7},{6,0},{7,1},{8,10},{9,11},{10,... | collective-permute-start | bytes 196616 | tf_op jit(solution)/shard_map/ppermute | solution.py:210
  216.6 5.0 %collective-permute-start.25 = (f32[64,256]{1,0:T(8,128)S(1)}, f32[64,256]{1,0:T(8,128)S(1)}, u32[]{:S(2)}, u32[]{:S(2)}) collective-permute-start(f32[64,256]{1,0:T(8,128)S(1)} %fusion.5), channel_id=1, source_target_pairs={{0,8},{1,9},{2,10},{3,11},{4,12},{5,13},{6,14},{7,15}} | collective-permute-start | bytes 196616 | tf_op jit(solution)/shard_map/ppermute | solution.py:280
  221.5 1.6 collective-permute-start.29
  223.8 1.3 copy-start.5
  223.8 1.3 copy-start.8
  225.1 1.4 collective-permute-start.30
  226.5 1.0 copy-start.3
  227.4 0.9 copy-start.6
  228.4 0.9 copy-start.9
  231.6 18.2 %collective-permute-start.31 = (f32[2,64,512]{2,1,0:T(8,128)}, f32[2,64,512]{2,1,0:T(8,128)}, u32[]{:S(2)}, u32[]{:S(2)}) collective-permute-start(f32[2,64,512]{2,1,0:T(8,128)} %bitcast.33), channel_id=1, source_target_pairs={{16,24},{17,25},{18,26},{19,27},{20,28},{21,29},{22,30},{23,31}} | collective-permute-start | bytes 786440 | tf_op jit(solution)/shard_map/ppermute | solution.py:290
  249.8 1.0 copy-start.4
  250.7 0.9 copy-start.7
  251.7 0.9 copy-start.10
  (1 other events, 0.9 us)
Sparse Core Ops, SparseCore 0:
  35.7 66.3 all-reduce.2

commit v2 on v1

--- a/solution.py
+++ b/solution.py
@@ -120,9 +120,8 @@
 def split(value):
     return pl.pallas_call(
         split_kernel,
-        out_specs=[pl.BlockSpec(memory_space=pltpu.VMEM)] * 2,
         out_shape=[jax.ShapeDtypeStruct(value.shape, jnp.bfloat16)] * 2,
-        compiler_params=pltpu.CompilerParams(vmem_limit_bytes=12 * 1024 * 1024),
+        compiler_params=pltpu.CompilerParams(vmem_limit_bytes=VMEM_LIMIT),
     )(value)
 
 
@@ -159,37 +158,59 @@
     )(place, mine, theirs)
 
 
-def rows_kernel(tree, *refs):
-    out = refs[-1]
-    terms, matrices = jax.tree.unflatten(tree, refs[:-1])
+def times_into(out, by_row, both, high, pieces):
+    count = high.shape[0] // 2
+    first = 0
+    for piece_high, piece_low in pieces:
+        product = dot(both, piece_high)
+        product = product[: 2 * count] + product[2 * count :] + dot(high, piece_low)
+        width = product.shape[1] // 2
+        columns = slice(first, first + width)
+        real_part = product[:count, :width] - product[count:, width:]
+        imag_part = product[:count, width:] + product[count:, :width]
+        if by_row:
+            out[:, 0, columns] = real_part
+            out[:, 1, columns] = imag_part
+        else:
+            out[0, :, columns] = real_part
+            out[1, :, columns] = imag_part
+        first += width
+
+
+def rows_kernel(tree, fetched, *refs):
+    if fetched:
+        *refs, out, buffer, sems = refs
+        refs, sources = refs[:-fetched], refs[-fetched:]
+        copies = [pltpu.make_async_copy(source, buffer.at[i], sems.at[i]) for i, source in enumerate(sources)]
+        for copy in copies:
+            copy.start()
+    else:
+        *refs, out = refs
+    terms, pieces = jax.tree.unflatten(tree, refs)
     flat = whole_rows(terms[0])
     for term in terms[1:]:
         flat = flat + whole_rows(term)
-    count = flat.shape[0] // 2
     high, low = halves_of(flat)
     both = jnp.concatenate([high, low], 0)
-    for number, matrix in enumerate(matrices):
-        first = 0
-        for piece in matrix:
-            product = dot(both, piece[0][...])
-            product = product[: 2 * count] + product[2 * count :] + dot(high, piece[1][...])
-            width = product.shape[1] // 2
-            columns = slice(first, first + width)
-            out[number, 0, :, columns] = product[:count, :width] - product[count:, width:]
-            out[number, 1, :, columns] = product[:count, width:] + product[count:, :width]
-            first += width
-
-
-def rows_times(terms, matrices, count, bands):
-    flat, tree = jax.tree.flatten((terms, matrices))
-    in_vmem = pl.BlockSpec(memory_space=pltpu.VMEM)
+    times_into(out.at[fetched], fetched > 0, both, high, [(one[...], two[...]) for one, two in pieces])
+    for i in range(fetched):
+        copies[i].wait()
+        times_into(out.at[i], True, both, high, [halves_of(buffer[i])])
+
+
+def rows_times(terms, pieces, count, bands, fetched=()):
+    flat, tree = jax.tree.flatten((terms, pieces))
+    scratch = []
+    if fetched:
+        scratch = [pltpu.VMEM((len(fetched), bands, 2 * bands), jnp.float32), pltpu.SemaphoreType.DMA((len(fetched),))]
     return pl.pallas_call(
-        functools.partial(rows_kernel, tree),
-        in_specs=[in_vmem if one.dtype == jnp.bfloat16 else pl.BlockSpec() for one in flat],
-        out_shape=jax.ShapeDtypeStruct((len(matrices), 2, count, bands), jnp.float32),
-        compiler_params=pltpu.CompilerParams(vmem_limit_bytes=12 * 1024 * 1024),
+        functools.partial(rows_kernel, tree, len(fetched)),
+        in_specs=[pl.BlockSpec()] * len(flat) + [pl.BlockSpec(memory_space=pl.ANY)] * len(fetched),
+        out_shape=jax.ShapeDtypeStruct((len(fetched) + 1, *((count, 2) if fetched else (2, count)), bands), jnp.float32),
+        scratch_shapes=scratch,
+        compiler_params=pltpu.CompilerParams(vmem_limit_bytes=VMEM_LIMIT),
         cost_estimate=pl.CostEstimate(flops=0, bytes_accessed=0, transcendentals=0),
-    )(*flat)
+    )(*flat, *fetched)
 
 
 def packed(states, kpoint, first, width):
@@ -255,7 +276,7 @@
     before = own_margins[0]
     for k in range(1, last):
         rows = jnp.stack([before[:, :bands], before[:, bands:]], 0)
-        before = rows_times([[rows]], [[split(own_margins[k])]], bands, bands)[0]
+        before = rows_times([[rows]], [split(own_margins[k])], bands, bands)[0]
         before = jnp.concatenate([before[0], before[1]], 1)
         own_margins[k] = before
     left = split(after(before, arrivals[0]))
@@ -286,12 +307,10 @@
     eye_real = jnp.where((row_index == col_index) & (ka_place == 0), 1.0, 0.0).astype(jnp.float32)
     starts = [[jnp.stack([eye_real, jnp.zeros_like(eye_real)], 0)], received]
     for number in range(1, ka_width - 1):
-        line = rows_times(starts[-1:], [span], band_rows, bands)[0]
+        line = rows_times(starts[-1:], span, band_rows, bands)[0]
         starts.append([lax.ppermute(line, "ka", [(number, number + 1)])])
 
-    margins = [[split(margin)] for margin in own_margins[:-1]] + [[left]]
-    lines = rows_times(starts, margins + [span], band_rows, bands)
-    return jnp.moveaxis(lines, 1, 2)
+    return rows_times(starts, span, band_rows, bands, own_margins)
 
 
 def solution(mesh):

time: 264 us -> 265 us (level)
    unnamed x32 -> x34, local copies, waits for them, and re-layouts: 14.2 us -> 14.3 us
  transfers between devices with their start and end apart: 33 -> 33, of which waited for: 20 -> 22; matrix products, arithmetic and copies ran while one was open for 6% -> 6% of each run, Pallas kernels for 14% -> 14%
where the time goes in v2:
time: 265 us; the launch traced here: 263 us
  waiting for transfers between devices  141 us (53%)
  Pallas kernels  45.1 us (17%)
  starting transfers between devices  30 us (11%)
  local copies, waits for them, and re-layouts  26.4 us (10%)
  between operations  13.8 us (5%)
  other arithmetic  6.23 us (2%)
    psum x1, waiting for transfers between devices, shards(): own_margins = [lax.psum(term, 'pw') for term in terms]  66.1 us
    ppermute x18, waiting for transfers between devices, other_chip(): lax.ppermute(block, 'pw', [(i, (i + 2 * distance) % size) for i in range(...  42.8 us
    pallas_call x4, Pallas kernels, margin_section(): pl.pallas_call(functools.partial(margin_kernel, steps, len(other_specs) /...  36.1 us
    ppermute x18, starting transfers between devices, other_chip(): lax.ppermute(block, 'pw', [(i, (i + 2 * distance) % size) for i in range(...  22.9 us
    ppermute x2, waiting for transfers between devices, shards(): starts.append([lax.ppermute(line, 'ka', [(number, number + 1)])])  15.6 us
    unnamed x34, local copies, waits for them, and re-layouts  14.3 us
    ppermute x4, waiting for transfers between devices, send(): lax.ppermute(after(blocks[number], earlier) if earlier else blocks[number...  11.4 us
    pallas_call x3, Pallas kernels, rows_times(): pl.pallas_call(functools.partial(rows_kernel, tree, len(fetched)), in_spe...  6.74 us
  transfers between devices with their start and end apart: 33, of which 22 were waited for; matrix products, arithmetic and copies ran while one was open for 6% of the time, Pallas kernels for 14%

profile of v2, /device:TPU:6, one launch (start us, length us, event | category | flops | bytes accessed | tf_op | source)
XLA Modules:
  0.0 262.8 jit_solution(5797280795878964006)
XLA Ops:
  6.5 3.4 %slice_bitcast_fusion = bf16[256,4096]{1,0:T(8,128)(2,1)} fusion(bf16[2,512,4096]{2,1,0:T(8,128)(2,1)} %refs_2_.3), kind=kLoop, calls=%fused_computation.2 | loop fusion | bytes 4194304 | tf_op jit(solution)/shard_map/squeeze | solution.py:264
  10.5 3.1 %slice_bitcast_fusion.1 = bf16[256,4096]{1,0:T(8,128)(2,1)} fusion(bf16[2,512,4096]{2,1,0:T(8,128)(2,1)} %refs_1_.3), kind=kLoop, calls=%fused_computation.3 | loop fusion | bytes 4194304 | tf_op jit(solution)/shard_map/squeeze | solution.py:264
  13.6 1.4 collective-permute-start
  15.0 2.7 %slice_bitcast_fusion.3 = (bf16[128,4096]{1,0:T(8,128)(2,1)}, bf16[128,4096]{1,0:T(8,128)(2,1)S(1)}) fusion(bf16[2,512,4096]{2,1,0:T(8,128)(2,1)} %refs_1_.3), kind=kLoop, calls=%fused_computation.5 | loop fusion | bytes 4194304 | tf_op jit(solution)/shard_map/squeeze | solution.py:217
  17.7 13.6 %shard_map.28 = f32[512,1024]{1,0:T(8,128)} custom-call(bf16[2,512,4096]{2,1,0:T(8,128)(2,1)S(1)} %copy-done, bf16[2,512,4096]{2,1,0:T(8,128)(2,1)} %refs_2_.3, bf16[2,512,4096]{2,1,0:T(8,128)(2,1)S(1)} %copy-done, bf16[2,512,4096]{2,1,0:T(8,128)(2,1)} %refs_2_.3), custom_call_target="tpu_custom_call" | custom-call | tf_op jit(solution)/shard_map/pallas_call | solution.py:104
  31.3 2.8 %slice_bitcast_fusion.2 = (bf16[128,4096]{1,0:T(8,128)(2,1)}, bf16[128,4096]{1,0:T(8,128)(2,1)S(1)}) fusion(bf16[2,512,4096]{2,1,0:T(8,128)(2,1)} %refs_2_.3), kind=kLoop, calls=%fused_computation.4 | loop fusion | bytes 4194304 | tf_op jit(solution)/shard_map/squeeze | solution.py:217
  34.1 1.6 pad_maximum_fusion
  36.1 66.1 %all-reduce.3.cloned.1.call-done.value.refs_11_ = f32[512,1024]{1,0:T(8,128)} async-done(((f32[512,1024]{1,0:T(8,128)}), f32[512,1024]{1,0:T(8,128)}) %all-reduce.3.cloned.1.call-update) | async-done | bytes 2097168 | tf_op jit(solution)/shard_map/psum | solution.py:275
  102.2 1.4 copy-done.13
  104.6 1.6 copy-done.2
  106.5 1.3 copy-done.14
  107.8 9.5 %shard_map.30 = (f32[4,64,512]{2,1,0:T(8,128)S(1)}, f32[4,64,512]{2,1,0:T(8,128)S(1)}) custom-call(s32[1]{0:T(128)} %bitcast.refs_0_, bf16[2,512,4096]{2,1,0:T(8,128)(2,1)} %refs_1_.3, bf16[2,512,4096]{2,1,0:T(8,128)(2,1)} %refs_2_.3, bf16[256,4096]{1,0:T(8,128)(2,1)} %collective-permute-done.refs_3_, bf16[256,4096]{1,0:T(8,128)(2,1)S(1)} %copy-done.14, ...), custom_call_target="tpu_custom_call" | custom-call | tf_op jit(solution)/shard_map/pallas_call | solution.py:104
  117.4 3.1 %pad_maximum_fusion.1 = bf16[256,4096]{1,0:T(8,128)(2,1)} fusion(bf16[128,4096]{1,0:T(8,128)(2,1)} %get-tuple-element.55, bf16[128,4096]{1,0:T(8,128)(2,1)} %get-tuple-element.53), kind=kLoop, calls=%fused_computation.1 | loop fusion | flops 4194304 | bytes 4194304 | tf_op jit(solution)/shard_map/concatenate | solution.py:217
  120.6 1.1 add.113
  121.8 1.6 collective-permute-start.3
  123.4 2.2 collective-permute-start.5
  126.4 3.5 %collective-permute-done.3 = f32[64,512]{1,0:T(8,128)S(1)} collective-permute-done((f32[64,512]{1,0:T(8,128)S(1)}, f32[64,512]{1,0:T(8,128)S(1)}, u32[]{:S(2)}, u32[]{:S(2)}) %collective-permute-start.3) | collective-permute-done | bytes 131104 | tf_op jit(solution)/shard_map/ppermute | solution.py:231
  129.9 1.8 collective-permute-done.5
  131.8 6.2 %collective-permute-done.4 = f32[64,512]{1,0:T(8,128)S(1)} collective-permute-done((f32[64,512]{1,0:T(8,128)S(1)}, f32[64,512]{1,0:T(8,128)S(1)}, u32[]{:S(2)}, u32[]{:S(2)}) %collective-permute-start.4) | collective-permute-done | bytes 131104 | tf_op jit(solution)/shard_map/ppermute | solution.py:231
  138.0 1.7 collective-permute-start.9
  140.3 3.8 %collective-permute-done.9 = f32[64,512]{1,0:T(8,128)S(1)} collective-permute-done((f32[64,512]{1,0:T(8,128)S(1)}, f32[64,512]{1,0:T(8,128)S(1)}, u32[]{:S(2)}, u32[]{:S(2)}) %collective-permute-start.9) | collective-permute-done | bytes 131104 | tf_op jit(solution)/shard_map/ppermute | solution.py:231
  144.1 7.0 %collective-permute-done.8 = f32[64,512]{1,0:T(8,128)S(1)} collective-permute-done((f32[64,512]{1,0:T(8,128)S(1)}, f32[64,512]{1,0:T(8,128)S(1)}, u32[]{:S(2)}, u32[]{:S(2)}) %collective-permute-start.8) | collective-permute-done | bytes 131104 | tf_op jit(solution)/shard_map/ppermute | solution.py:231
  151.2 3.4 %copy-done.1 = bf16[2,512,4096]{2,1,0:T(8,128)(2,1)S(1)} copy-done((bf16[2,512,4096]{2,1,0:T(8,128)(2,1)S(1)}, bf16[2,512,4096]{2,1,0:T(8,128)(2,1)}, u32[]{:S(2)}) %copy-start.1) | copy-done | bytes 8388632
  154.6 6.5 %shard_map.31 = (f32[4,64,256]{2,1,0:T(8,128)S(1)}, f32[4,64,256]{2,1,0:T(8,128)S(1)}) custom-call(s32[1]{0:T(128)} %bitcast.refs_0_, bf16[2,512,4096]{2,1,0:T(8,128)(2,1)S(1)} %copy-done.1, bf16[2,512,4096]{2,1,0:T(8,128)(2,1)} %refs_2_.3, bf16[256,4096]{1,0:T(8,128)(2,1)} %collective-permute-done.6.refs_3_.refs_4_, ...), custom_call_target="tpu_custom_call" | custom-call | tf_op jit(solution)/shard_map/pallas_call | solution.py:104
  161.1 1.5 collective-permute-done.10
  163.2 3.4 %collective-permute-start.13 = (f32[64,256]{1,0:T(8,128)S(1)}, f32[64,256]{1,0:T(8,128)S(1)}, u32[]{:S(2)}, u32[]{:S(2)}) collective-permute-start(f32[64,256]{1,0:T(8,128)S(1)} %get-tuple-element.64), channel_id=1, source_target_pairs={{0,6},{1,7},{2,0},{3,1},{4,2},{5,3},{6,4},{7,5},{8,14},{9,15},{10,... | collective-permute-start | bytes 196616 | tf_op jit(solution)/shard_map/ppermute | solution.py:231
  167.2 2.3 collective-permute-done.11
  169.5 3.4 %collective-permute-done.12 = f32[64,256]{1,0:T(8,128)S(1)} collective-permute-done((f32[64,256]{1,0:T(8,128)S(1)}, f32[64,256]{1,0:T(8,128)S(1)}, u32[]{:S(2)}, u32[]{:S(2)}) %collective-permute-start.12) | collective-permute-done | bytes 65568 | tf_op jit(solution)/shard_map/ppermute | solution.py:231
  173.0 2.1 collective-permute-start.16
  175.1 1.8 collective-permute-start.18
  176.9 3.2 %collective-permute-done.17 = f32[64,256]{1,0:T(8,128)S(1)} collective-permute-done((f32[64,256]{1,0:T(8,128)S(1)}, f32[64,256]{1,0:T(8,128)S(1)}, u32[]{:S(2)}, u32[]{:S(2)}) %collective-permute-start.17) | collective-permute-done | bytes 65568 | tf_op jit(solution)/shard_map/ppermute | solution.py:231
  182.9 10.4 %collective-permute-done.14.refs_3_.refs_4_ = bf16[256,4096]{1,0:T(8,128)(2,1)} collective-permute-done((bf16[256,4096]{1,0:T(8,128)(2,1)}, bf16[256,4096]{1,0:T(8,128)(2,1)}, u32[]{:S(2)}, u32[]{:S(2)}) %collective-permute-start.14) | collective-permute-done | bytes 2097184 | tf_op jit(solution)/shard_map/ppermute | solution.py:268
  194.2 6.5 %shard_map.34 = (f32[4,64,256]{2,1,0:T(8,128)S(1)}, f32[4,64,256]{2,1,0:T(8,128)S(1)}) custom-call(s32[1]{0:T(128)} %bitcast.refs_0_, bf16[2,512,4096]{2,1,0:T(8,128)(2,1)S(1)} %copy-done.1, bf16[2,512,4096]{2,1,0:T(8,128)(2,1)} %refs_2_.3, bf16[256,4096]{1,0:T(8,128)(2,1)} %collective-permute-done.14.refs_3_.refs_4_, ...), custom_call_target="tpu_custom_call" | custom-call | tf_op jit(solution)/shard_map/pallas_call | solution.py:104
  200.8 1.5 collective-permute-done.21
  202.4 1.6 collective-permute-start.22
  204.0 2.2 collective-permute-start.24
  207.1 1.6 collective-permute-done.22
  209.3 3.4 %collective-permute-done.23 = f32[64,256]{1,0:T(8,128)S(1)} collective-permute-done((f32[64,256]{1,0:T(8,128)S(1)}, f32[64,256]{1,0:T(8,128)S(1)}, u32[]{:S(2)}, u32[]{:S(2)}) %collective-permute-start.23) | collective-permute-done | bytes 65568 | tf_op jit(solution)/shard_map/ppermute | solution.py:231
  212.7 2.3 collective-permute-start.28
  216.2 1.2 collective-permute-done.28
  217.4 4.2 %collective-permute-done.27 = f32[64,256]{1,0:T(8,128)S(1)} collective-permute-done((f32[64,256]{1,0:T(8,128)S(1)}, f32[64,256]{1,0:T(8,128)S(1)}, u32[]{:S(2)}, u32[]{:S(2)}) %collective-permute-start.27) | collective-permute-done | bytes 65568 | tf_op jit(solution)/shard_map/ppermute | solution.py:231
  221.8 1.5 collective-permute-done.29.theirs
  224.0 1.3 shard_map.36
  225.3 1.5 collective-permute-start.30
  229.6 2.2 shard_map.37
  231.9 1.3 collective-permute-start.31
  233.3 15.6 %collective-permute-done.31.refs_4_ = f32[2,64,512]{2,1,0:T(8,128)} collective-permute-done((f32[2,64,512]{2,1,0:T(8,128)}, f32[2,64,512]{2,1,0:T(8,128)}, u32[]{:S(2)}, u32[]{:S(2)}) %collective-permute-start.31) | collective-permute-done | bytes 262176 | tf_op jit(solution)/shard_map/ppermute | solution.py:311
  252.7 3.2 %shard_map.38 = f32[2,64,2,512]{3,2,1,0:T(2,128)} custom-call(f32[2,64,512]{2,1,0:T(8,128)S(1)} %stack.56.refs_0_, f32[64,768]{1,0:T(8,128)S(1)} %copy-done.16, f32[64,256]{1,0:T(8,128)S(1)} %collective-permute-done.25.refs_1_.refs_2_, f32[2,64,512]{2,1,0:T(8,128)} %collective-permute-done.30.refs_0_.refs_3_, f32[2,64,512]{2,1,0:T(8,128)} %collective-permute-done.31.refs_4_, ...), custom_call_target="tpu_custom_call" | custom-call | tf_op jit(solution)/shard_map/pallas_call | solution.py:206
  (89 shorter events, 19.2 us)
Async XLA Ops:
  6.5 95.6 %all-reduce.3.cloned.1.call-start = ((), (), s32[]{:S(2)}) async-start(), calls=%async_computation | async-start | bytes 4194304 | tf_op jit(solution)/shard_map/psum | solution.py:275
  6.5 11.2 %copy-start = (bf16[2,512,4096]{2,1,0:T(8,128)(2,1)S(1)}, bf16[2,512,4096]{2,1,0:T(8,128)(2,1)}, u32[]{:S(2)}) copy-start(bf16[2,512,4096]{2,1,0:T(8,128)(2,1)} %refs_1_.3) | copy-start | bytes 25165828
  9.9 92.3 %collective-permute-start.1 = (bf16[256,4096]{1,0:T(8,128)(2,1)}, bf16[256,4096]{1,0:T(8,128)(2,1)S(1)}, u32[]{:S(2)}, u32[]{:S(2)}) collective-permute-start(bf16[256,4096]{1,0:T(8,128)(2,1)} %slice_bitcast_fusion), channel_id=1, source_target_pairs={{0,24},{8,0},{16,8},{24,16},{1,25},{9,1},{17,9},{25,17},{2,26},{10... | collective-permute-start | bytes 6291464 | tf_op jit(solution)/shard_map/ppermute | solution.py:268
  13.6 91.0 %collective-permute-start = (bf16[256,4096]{1,0:T(8,128)(2,1)}, bf16[256,4096]{1,0:T(8,128)(2,1)}, u32[]{:S(2)}, u32[]{:S(2)}) collective-permute-start(bf16[256,4096]{1,0:T(8,128)(2,1)} %slice_bitcast_fusion.1), channel_id=1, source_target_pairs={{0,24},{8,0},{16,8},{24,16},{1,25},{9,1},{17,9},{25,17},{2,26},{10... | collective-permute-start | bytes 6291464 | tf_op jit(solution)/shard_map/ppermute | solution.py:268
  35.7 115.5 %collective-permute-start.6 = (bf16[256,4096]{1,0:T(8,128)(2,1)}, bf16[256,4096]{1,0:T(8,128)(2,1)}, u32[]{:S(2)}, u32[]{:S(2)}) collective-permute-start(bf16[256,4096]{1,0:T(8,128)(2,1)} %pad_maximum_fusion), channel_id=1, source_target_pairs={{0,24},{8,0},{16,8},{24,16},{1,25},{9,1},{17,9},{25,17},{2,26},{10... | collective-permute-start | bytes 6291464 | tf_op jit(solution)/shard_map/ppermute | solution.py:268
  102.2 1.4 copy-start.13
  104.6 1.6 copy-start.2
  106.2 1.6 copy-start.14
  117.3 3.3 %collective-permute-start.2 = (f32[4,64,512]{2,1,0:T(8,128)S(1)}, f32[4,64,512]{2,1,0:T(8,128)}, u32[]{:S(2)}, u32[]{:S(2)}) collective-permute-start(f32[4,64,512]{2,1,0:T(8,128)S(1)} %get-tuple-element.35), channel_id=1, source_target_pairs={{0,1},{1,0},{2,3},{3,2},{4,5},{5,4},{6,7},{7,6},{8,9},{9,8},{10,11... | collective-permute-start | bytes 1572872 | tf_op jit(solution)/shard_map/ppermute | solution.py:226
  120.6 72.7 %collective-permute-start.14 = (bf16[256,4096]{1,0:T(8,128)(2,1)}, bf16[256,4096]{1,0:T(8,128)(2,1)}, u32[]{:S(2)}, u32[]{:S(2)}) collective-permute-start(bf16[256,4096]{1,0:T(8,128)(2,1)} %pad_maximum_fusion.1), channel_id=1, source_target_pairs={{0,24},{8,0},{16,8},{24,16},{1,25},{9,1},{17,9},{25,17},{2,26},{10... | collective-permute-start | bytes 6291464 | tf_op jit(solution)/shard_map/ppermute | solution.py:268
  121.8 8.2 %collective-permute-start.3 = (f32[64,512]{1,0:T(8,128)S(1)}, f32[64,512]{1,0:T(8,128)S(1)}, u32[]{:S(2)}, u32[]{:S(2)}) collective-permute-start(f32[64,512]{1,0:T(8,128)S(1)} %get-tuple-element.57), channel_id=1, source_target_pairs={{0,2},{1,3},{2,4},{3,5},{4,6},{5,7},{6,0},{7,1},{8,10},{9,11},{10,... | collective-permute-start | bytes 393224 | tf_op jit(solution)/shard_map/ppermute | solution.py:231
  123.4 8.4 %collective-permute-start.5 = (f32[64,512]{1,0:T(8,128)S(1)}, f32[64,512]{1,0:T(8,128)S(1)}, u32[]{:S(2)}, u32[]{:S(2)}) collective-permute-start(f32[64,512]{1,0:T(8,128)S(1)} %get-tuple-element.58), channel_id=1, source_target_pairs={{0,6},{1,7},{2,0},{3,1},{4,2},{5,3},{6,4},{7,5},{8,14},{9,15},{10,... | collective-permute-start | bytes 393224 | tf_op jit(solution)/shard_map/ppermute | solution.py:231
  125.6 12.3 %collective-permute-start.4 = (f32[64,512]{1,0:T(8,128)S(1)}, f32[64,512]{1,0:T(8,128)S(1)}, u32[]{:S(2)}, u32[]{:S(2)}) collective-permute-start(f32[64,512]{1,0:T(8,128)S(1)} %get-tuple-element.59), channel_id=1, source_target_pairs={{0,4},{1,5},{2,6},{3,7},{4,0},{5,1},{6,2},{7,3},{8,12},{9,13},{10,... | collective-permute-start | bytes 393224 | tf_op jit(solution)/shard_map/ppermute | solution.py:231
  138.0 6.1 %collective-permute-start.9 = (f32[64,512]{1,0:T(8,128)S(1)}, f32[64,512]{1,0:T(8,128)S(1)}, u32[]{:S(2)}, u32[]{:S(2)}) collective-permute-start(f32[64,512]{1,0:T(8,128)S(1)} %fusion.1), channel_id=1, source_target_pairs={{0,6},{1,7},{2,0},{3,1},{4,2},{5,3},{6,4},{7,5},{8,14},{9,15},{10,... | collective-permute-start | bytes 393224 | tf_op jit(solution)/shard_map/ppermute | solution.py:231
  139.7 11.5 %collective-permute-start.8 = (f32[64,512]{1,0:T(8,128)S(1)}, f32[64,512]{1,0:T(8,128)S(1)}, u32[]{:S(2)}, u32[]{:S(2)}) collective-permute-start(f32[64,512]{1,0:T(8,128)S(1)} %fusion.1), channel_id=1, source_target_pairs={{0,4},{1,5},{2,6},{3,7},{4,0},{5,1},{6,2},{7,3},{8,12},{9,13},{10,... | collective-permute-start | bytes 393224 | tf_op jit(solution)/shard_map/ppermute | solution.py:231
  139.7 11.5 %collective-permute-start.7 = (f32[64,512]{1,0:T(8,128)S(1)}, f32[64,512]{1,0:T(8,128)S(1)}, u32[]{:S(2)}, u32[]{:S(2)}) collective-permute-start(f32[64,512]{1,0:T(8,128)S(1)} %fusion.1), channel_id=1, source_target_pairs={{0,2},{1,3},{2,4},{3,5},{4,6},{5,7},{6,0},{7,1},{8,10},{9,11},{10,... | collective-permute-start | bytes 393224 | tf_op jit(solution)/shard_map/ppermute | solution.py:231
  151.2 3.4 %copy-start.1 = (bf16[2,512,4096]{2,1,0:T(8,128)(2,1)S(1)}, bf16[2,512,4096]{2,1,0:T(8,128)(2,1)}, u32[]{:S(2)}) copy-start(bf16[2,512,4096]{2,1,0:T(8,128)(2,1)} %refs_1_.3) | copy-start | bytes 25165828
  161.0 1.6 collective-permute-start.10
  162.7 6.8 %collective-permute-start.11 = (f32[64,256]{1,0:T(8,128)S(1)}, f32[64,256]{1,0:T(8,128)S(1)}, u32[]{:S(2)}, u32[]{:S(2)}) collective-permute-start(f32[64,256]{1,0:T(8,128)S(1)} %get-tuple-element.63), channel_id=1, source_target_pairs={{0,2},{1,3},{2,4},{3,5},{4,6},{5,7},{6,0},{7,1},{8,10},{9,11},{10,... | collective-permute-start | bytes 196616 | tf_op jit(solution)/shard_map/ppermute | solution.py:231
  163.2 6.4 %collective-permute-start.13 = (f32[64,256]{1,0:T(8,128)S(1)}, f32[64,256]{1,0:T(8,128)S(1)}, u32[]{:S(2)}, u32[]{:S(2)}) collective-permute-start(f32[64,256]{1,0:T(8,128)S(1)} %get-tuple-element.64), channel_id=1, source_target_pairs={{0,6},{1,7},{2,0},{3,1},{4,2},{5,3},{6,4},{7,5},{8,14},{9,15},{10,... | collective-permute-start | bytes 196616 | tf_op jit(solution)/shard_map/ppermute | solution.py:231
  166.6 6.3 %collective-permute-start.12 = (f32[64,256]{1,0:T(8,128)S(1)}, f32[64,256]{1,0:T(8,128)S(1)}, u32[]{:S(2)}, u32[]{:S(2)}) collective-permute-start(f32[64,256]{1,0:T(8,128)S(1)} %get-tuple-element.65), channel_id=1, source_target_pairs={{0,4},{1,5},{2,6},{3,7},{4,0},{5,1},{6,2},{7,3},{8,12},{9,13},{10,... | collective-permute-start | bytes 196616 | tf_op jit(solution)/shard_map/ppermute | solution.py:231
  167.2 13.6 %collective-permute-start.15 = (f32[4,64,512]{2,1,0:T(8,128)S(1)}, f32[4,64,512]{2,1,0:T(8,128)S(1)}, u32[]{:S(2)}, u32[]{:S(2)}) collective-permute-start(f32[4,64,512]{2,1,0:T(8,128)S(1)} %pad_maximum_fusion.2.mine), channel_id=1, source_target_pairs={{0,1},{1,0},{2,3},{3,2},{4,5},{5,4},{6,7},{7,6},{8,9},{9,8},{10,11... | collective-permute-start | bytes 1572872 | tf_op jit(solution)/shard_map/ppermute | solution.py:226
  172.9 7.2 %collective-permute-start.17 = (f32[64,256]{1,0:T(8,128)S(1)}, f32[64,256]{1,0:T(8,128)S(1)}, u32[]{:S(2)}, u32[]{:S(2)}) collective-permute-start(f32[64,256]{1,0:T(8,128)S(1)} %fusion.7), channel_id=1, source_target_pairs={{0,4},{1,5},{2,6},{3,7},{4,0},{5,1},{6,2},{7,3},{8,12},{9,13},{10,... | collective-permute-start | bytes 196616 | tf_op jit(solution)/shard_map/ppermute | solution.py:231
  173.0 7.1 %collective-permute-start.16 = (f32[64,256]{1,0:T(8,128)S(1)}, f32[64,256]{1,0:T(8,128)S(1)}, u32[]{:S(2)}, u32[]{:S(2)}) collective-permute-start(f32[64,256]{1,0:T(8,128)S(1)} %fusion.7), channel_id=1, source_target_pairs={{0,2},{1,3},{2,4},{3,5},{4,6},{5,7},{6,0},{7,1},{8,10},{9,11},{10,... | collective-permute-start | bytes 196616 | tf_op jit(solution)/shard_map/ppermute | solution.py:231
  175.1 5.5 %collective-permute-start.18 = (f32[64,256]{1,0:T(8,128)S(1)}, f32[64,256]{1,0:T(8,128)S(1)}, u32[]{:S(2)}, u32[]{:S(2)}) collective-permute-start(f32[64,256]{1,0:T(8,128)S(1)} %fusion.7), channel_id=1, source_target_pairs={{0,6},{1,7},{2,0},{3,1},{4,2},{5,3},{6,4},{7,5},{8,14},{9,15},{10,... | collective-permute-start | bytes 196616 | tf_op jit(solution)/shard_map/ppermute | solution.py:231
  180.7 1.6 collective-permute-start.19
  182.9 41.1 %copy-start.4 = (bf16[512,256]{1,0:T(8,128)(2,1)}, bf16[512,256]{1,0:T(8,128)(2,1)S(1)}, u32[]{:S(2)}) copy-start(bf16[512,256]{1,0:T(8,128)(2,1)S(1)} %get-tuple-element.44.refs_5_.refs_4_.refs_8_) | copy-start | bytes 786436
  193.3 7.4 %collective-permute-start.20 = (f32[64,768]{1,0:T(8,128)S(1)}, f32[64,768]{1,0:T(8,128)S(1)}, u32[]{:S(2)}, u32[]{:S(2)}) collective-permute-start(f32[64,768]{1,0:T(8,128)S(1)} %pad_maximum_fusion.5), channel_id=1, source_target_pairs={{0,8},{1,9},{2,10},{3,11},{4,12},{5,13},{6,14},{7,15}} | collective-permute-start | bytes 589832 | tf_op jit(solution)/shard_map/ppermute | solution.py:292
  200.7 24.6 %copy-start.15 = (f32[64,768]{1,0:T(8,128)}, f32[64,768]{1,0:T(8,128)S(1)}, u32[]{:S(2)}) copy-start(f32[64,768]{1,0:T(8,128)S(1)} %collective-permute-done.20.refs_0_.refs_1_) | copy-start | bytes 589828
  200.7 1.6 collective-permute-start.21
  202.4 6.2 %collective-permute-start.22 = (f32[64,256]{1,0:T(8,128)S(1)}, f32[64,256]{1,0:T(8,128)S(1)}, u32[]{:S(2)}, u32[]{:S(2)}) collective-permute-start(f32[64,256]{1,0:T(8,128)S(1)} %get-tuple-element.60), channel_id=1, source_target_pairs={{0,2},{1,3},{2,4},{3,5},{4,6},{5,7},{6,0},{7,1},{8,10},{9,11},{10,... | collective-permute-start | bytes 196616 | tf_op jit(solution)/shard_map/ppermute | solution.py:231
  204.0 5.3 %collective-permute-start.24 = (f32[64,256]{1,0:T(8,128)S(1)}, f32[64,256]{1,0:T(8,128)S(1)}, u32[]{:S(2)}, u32[]{:S(2)}) collective-permute-start(f32[64,256]{1,0:T(8,128)S(1)} %get-tuple-element.61), channel_id=1, source_target_pairs={{0,6},{1,7},{2,0},{3,1},{4,2},{5,3},{6,4},{7,5},{8,14},{9,15},{10,... | collective-permute-start | bytes 196616 | tf_op jit(solution)/shard_map/ppermute | solution.py:231
  206.3 6.4 %collective-permute-start.23 = (f32[64,256]{1,0:T(8,128)S(1)}, f32[64,256]{1,0:T(8,128)S(1)}, u32[]{:S(2)}, u32[]{:S(2)}) collective-permute-start(f32[64,256]{1,0:T(8,128)S(1)} %get-tuple-element.62), channel_id=1, source_target_pairs={{0,4},{1,5},{2,6},{3,7},{4,0},{5,1},{6,2},{7,3},{8,12},{9,13},{10,... | collective-permute-start | bytes 196616 | tf_op jit(solution)/shard_map/ppermute | solution.py:231
  212.7 4.8 %collective-permute-start.28 = (f32[64,256]{1,0:T(8,128)S(1)}, f32[64,256]{1,0:T(8,128)S(1)}, u32[]{:S(2)}, u32[]{:S(2)}) collective-permute-start(f32[64,256]{1,0:T(8,128)S(1)} %fusion.5), channel_id=1, source_target_pairs={{0,6},{1,7},{2,0},{3,1},{4,2},{5,3},{6,4},{7,5},{8,14},{9,15},{10,... | collective-permute-start | bytes 196616 | tf_op jit(solution)/shard_map/ppermute | solution.py:231
  214.9 6.7 %collective-permute-start.27 = (f32[64,256]{1,0:T(8,128)S(1)}, f32[64,256]{1,0:T(8,128)S(1)}, u32[]{:S(2)}, u32[]{:S(2)}) collective-permute-start(f32[64,256]{1,0:T(8,128)S(1)} %fusion.5), channel_id=1, source_target_pairs={{0,4},{1,5},{2,6},{3,7},{4,0},{5,1},{6,2},{7,3},{8,12},{9,13},{10,... | collective-permute-start | bytes 196616 | tf_op jit(solution)/shard_map/ppermute | solution.py:231
  214.9 6.7 %collective-permute-start.26 = (f32[64,256]{1,0:T(8,128)S(1)}, f32[64,256]{1,0:T(8,128)S(1)}, u32[]{:S(2)}, u32[]{:S(2)}) collective-permute-start(f32[64,256]{1,0:T(8,128)S(1)} %fusion.5), channel_id=1, source_target_pairs={{0,2},{1,3},{2,4},{3,5},{4,6},{5,7},{6,0},{7,1},{8,10},{9,11},{10,... | collective-permute-start | bytes 196616 | tf_op jit(solution)/shard_map/ppermute | solution.py:231
  215.6 6.1 %collective-permute-start.25 = (f32[64,256]{1,0:T(8,128)S(1)}, f32[64,256]{1,0:T(8,128)S(1)}, u32[]{:S(2)}, u32[]{:S(2)}) collective-permute-start(f32[64,256]{1,0:T(8,128)S(1)} %fusion.5), channel_id=1, source_target_pairs={{0,8},{1,9},{2,10},{3,11},{4,12},{5,13},{6,14},{7,15}} | collective-permute-start | bytes 196616 | tf_op jit(solution)/shard_map/ppermute | solution.py:301
  221.7 1.6 collective-permute-start.29
  224.0 1.3 copy-start.7
  224.0 1.3 copy-start.10
  225.3 23.7 %copy-start.3 = (f32[512,1024]{1,0:T(8,128)S(1)}, f32[512,1024]{1,0:T(8,128)}, u32[]{:S(2)}) copy-start(f32[512,1024]{1,0:T(8,128)} %all-reduce.3.cloned.1.call-done.value.refs_11_) | copy-start | bytes 6291460
  225.3 1.5 collective-permute-start.30
  226.8 1.0 copy-start.5
  227.7 0.9 copy-start.8
  228.7 0.9 copy-start.11
  231.9 17.1 %collective-permute-start.31 = (f32[2,64,512]{2,1,0:T(8,128)}, f32[2,64,512]{2,1,0:T(8,128)}, u32[]{:S(2)}, u32[]{:S(2)}) collective-permute-start(f32[2,64,512]{2,1,0:T(8,128)} %bitcast.33), channel_id=1, source_target_pairs={{16,24},{17,25},{18,26},{19,27},{20,28},{21,29},{22,30},{23,31}} | collective-permute-start | bytes 786440 | tf_op jit(solution)/shard_map/ppermute | solution.py:311
  248.9 1.0 copy-start.6
  249.9 0.9 copy-start.9
  (2 other events, 1.9 us)
Sparse Core Ops, SparseCore 0:
  35.8 66.3 all-reduce.2
